TPU v7x, 512 devices: a whole 4x8x8 slice. The times are simulated.
512 devices in a mesh: cell: 64 (over z, x, core), gene: 8 (over y).
Axes of the slice: x: 4, y: 8, z: 8, core: 2. Of those that a mesh axis runs over, the one named last changes fastest.
Arguments:
- expression: bfloat16 [36864, 4096], P('cell', 'gene'), may hold values from -6 to 6
- gene_mean: float32 [4096], P('gene'), may hold values from -0.5 to 0.5
- loadings: bfloat16 [4096, 256], P('gene'), may hold values from -0.09375 to 0.09375
- nbr_index: int32 [36864, 30], P('cell'), may hold values from 0 to 36863, as said below
- nbr_count: int32 [36864], P('cell'), may hold values from 8 to 30
- nbr_weight: float32 [36864, 30], P('cell'), may hold values from 0.1 to 1
- batch: int32 [36864], P('cell'), may hold values from 0 to 15
- centroids: float32 [1000, 256], replicated, may hold values from -6 to 6
Outputs:
- smooth: float32 [36864, 256], P('cell', 'gene')
- new_centroids: float32 [1000, 256], replicated
- final_obs: float32 [1000, 16], replicated
Inputs may be any that keep to these rules, and one draw needn't show every extreme that they name: `nbr_index`: every entry differs from its row's cell index by 1 to 576, and the distance 576 occurs.
All inputs are finite; a program needn't handle non-finite values.
Results may differ from a plain program's by a relative error of at most 0.0022.
The roundings to bfloat16 on the way count: a program that leaves them out, or rounds other values in their place, can miss the bound.
Values sent between devices are 32-bit elements; how exact they have to be, the bound alone decides.
A program may use at most 64 MiB of HBM per device.

v0:
```python
import jax
import jax.numpy as jnp
from jax import lax
from jax.sharding import PartitionSpec as P

B = 16
NBR = 30
DIFF_STEPS = 3


EPSILON = 1e-06
SIGMA_SCALE = 0.1


def with_halo(x, sides, width):
    for axis, dim in sides:
        size, length = (lax.axis_size(axis), x.shape[dim])
        up = [(i, (i + 1) % size) for i in range(size - 1)]
        down = [(j, i) for i, j in up]
        last = lax.slice_in_dim(x, length - width, length, axis=dim)
        initial = lax.slice_in_dim(x, 0, width, axis=dim)
        before = lax.ppermute(last, axis, up)
        after = lax.ppermute(initial, axis, down)
        x = jnp.concatenate([before, x, after], axis=dim)
    return x


def diffuse_block(state_field, local_index, weights, denominator, row_count):
    padded = with_halo(state_field, (("cell", 0),), row_count)

    def add_slot(slot, total_sum):
        column = lax.dynamic_slice_in_dim(local_index, slot, 1, 1)[:, 0]
        weight = lax.dynamic_slice_in_dim(weights, slot, 1, 1)
        return total_sum + weight * jnp.take(padded, column, axis=0)

    total_sum = lax.fori_loop(0, NBR, add_slot, state_field)
    return total_sum / denominator[:, None]


def first_pass(full_rows, own_batch, centroids):
    row_norm = jnp.sqrt(jnp.sum(full_rows * full_rows, axis=1, keepdims=True) + EPSILON)
    unit_rows = (full_rows / row_norm).astype(jnp.bfloat16)
    cent_norm = jnp.sqrt(jnp.sum(centroids * centroids, axis=1, keepdims=True) + EPSILON)
    cent_unit = (centroids / cent_norm).astype(jnp.bfloat16)
    scores = jnp.dot(unit_rows, cent_unit.T, preferred_element_type=jnp.float32)
    kernel = jnp.exp((scores - 1.0) * (2.0 / SIGMA_SCALE))
    first_resp = kernel / jnp.sum(kernel, axis=1, keepdims=True)
    onehot = (own_batch[:, None] == jnp.arange(B)[None, :]).astype(jnp.float32)
    first_obs = lax.dot_general(
        first_resp, onehot, (((0,), (0,)), ((), ())), precision=lax.Precision.HIGHEST
    )
    batch_sizes = jnp.sum(onehot, axis=0)
    return (unit_rows, kernel, onehot, first_obs, batch_sizes)


def second_pass(unit_rows, kernel, onehot, first_obs, batch_sizes):
    expect = jnp.sum(first_obs, axis=1, keepdims=True) * batch_sizes[None, :] / jnp.sum(batch_sizes)
    ratio = (expect + 1.0) / (first_obs + 1.0)
    penalty = ratio * ratio
    factor = jnp.dot(onehot, penalty.T, precision=lax.Precision.HIGHEST)
    weighted = kernel * factor
    response = (weighted / jnp.sum(weighted, axis=1, keepdims=True)).astype(jnp.bfloat16)
    cent_sums = lax.dot_general(
        response, unit_rows, (((0,), (0,)), ((), ())), preferred_element_type=jnp.float32
    )
    final_obs = lax.dot_general(
        response,
        onehot.astype(jnp.bfloat16),
        (((0,), (0,)), ((), ())),
        preferred_element_type=jnp.float32,
    )
    return (cent_sums, final_obs)


def shards(expression, gene_mean, loadings, nbr_index, nbr_count, nbr_weight, batch, centroids):
    row_count = expression.shape[0]
    gene_count = lax.axis_size("gene")
    gene_index = lax.axis_index("gene")
    share_cols = loadings.shape[1] // gene_count
    mean_proj = jnp.dot(gene_mean, loadings.astype(jnp.float32), precision=lax.Precision.HIGHEST)
    partial_value = (
        jnp.dot(expression, loadings, preferred_element_type=jnp.float32) - mean_proj[None, :]
    )
    state_field = lax.psum(partial_value, "gene")
    block_start = lax.axis_index("cell") * row_count
    local_index = nbr_index - block_start + row_count
    live_slots = jnp.arange(NBR)[None, :] < nbr_count[:, None]
    weights = jnp.where(live_slots, nbr_weight, jnp.float32(0.0))
    denominator = 1.0 + jnp.sum(weights, axis=1)
    for repeat_step in range(DIFF_STEPS):
        state_field = diffuse_block(state_field, local_index, weights, denominator, row_count)
    smooth_out = lax.dynamic_slice_in_dim(state_field, gene_index * share_cols, share_cols, 1)
    unit_rows, kernel, onehot, first_obs, batch_sizes = first_pass(state_field, batch, centroids)
    first_obs, batch_sizes = lax.psum((first_obs, batch_sizes), "cell")
    cent_sums, final_obs = second_pass(unit_rows, kernel, onehot, first_obs, batch_sizes)
    cent_sums, final_obs = lax.psum((cent_sums, final_obs), "cell")
    new_centroids = cent_sums / jnp.sqrt(
        jnp.sum(cent_sums * cent_sums, axis=1, keepdims=True) + EPSILON
    )
    return (smooth_out, new_centroids, final_obs)


def solution(mesh):
    in_specs = (
        P("cell", "gene"),
        P("gene"),
        P("gene", None),
        P("cell", None),
        P("cell"),
        P("cell", None),
        P("cell"),
        P(),
    )
    out_specs = (P("cell", "gene"), P(), P())
    return jax.shard_map(shards, mesh=mesh, in_specs=in_specs, out_specs=out_specs, check_vma=False)
```

profile of v0, /device:TPU:256, one launch (start us, length us, event | category | flops | bytes accessed | tf_op | source)
XLA Modules:
  0.0 1025.1 jit_solution(10102806802913338869)
XLA Ops:
  10.7 81.2 %all-reduce.4.cloned.1.call-done = f32[576,256]{1,0:T(8,128)} async-done(((f32[576,256]{1,0:T(8,128)}), f32[576,256]{1,0:T(8,128)}) %all-reduce.4.cloned.1.call-update) | async-done | bytes 589840 | tf_op jit(solution)/shard_map/psum | solution.py:84
  93.8 2.4 collective-permute-start
  98.1 3.4 collective-permute-done.1
  101.5 7.0 collective-permute-done
  109.7 120.5 %while.39 = (s32[]{:T(128)}, f32[576,256]{1,0:T(8,128)S(1)}, f32[576,30]{0,1:T(8,128)}, s32[576,30]{0,1:T(8,128)}, f32[1728,256]{1,0:T(8,128)S(1)}, /*index=5*/s32[]{:T(128)}) while((s32[]{:T(128)}, f32[576,256]{1,0:T(8,128)S(1)}, f32[576,30]{0,1:T(8,128)}, s32[576,30]{0,1:T(8,128)}, f32[1728,256]{1,0:T(8,128)S(1)}, ...), condition=%wide.region_2.4_spmd, body=%wide.region_1.0_spmd.sunk | while | flops 448578 | bytes 2977493 | solution.py:36
  111.3 2.2 gather_fusion
  115.3 2.2 gather_fusion
  119.3 2.2 gather_fusion
  123.3 2.2 gather_fusion
  127.3 2.2 gather_fusion
  131.4 2.2 gather_fusion
  135.4 2.2 gather_fusion
  139.4 2.2 gather_fusion
  151.5 2.2 gather_fusion
  159.5 2.2 gather_fusion
  167.5 2.2 gather_fusion
  179.6 2.2 gather_fusion
  187.6 2.2 gather_fusion
  195.6 2.2 gather_fusion
  199.7 2.2 gather_fusion
  207.7 2.2 gather_fusion
  215.7 2.2 gather_fusion
  227.8 2.2 gather_fusion
  232.3 2.4 collective-permute-start.2
  234.8 5.0 collective-permute-done.3
  239.7 7.2 collective-permute-done.2
  248.1 120.5 %while.40 = (s32[]{:T(128)}, f32[576,256]{1,0:T(8,128)S(1)}, f32[576,30]{0,1:T(8,128)}, s32[576,30]{0,1:T(8,128)}, f32[1728,256]{1,0:T(8,128)S(1)}, /*index=5*/s32[]{:T(128)}) while((s32[]{:T(128)}, f32[576,256]{1,0:T(8,128)S(1)}, f32[576,30]{0,1:T(8,128)}, s32[576,30]{0,1:T(8,128)}, f32[1728,256]{1,0:T(8,128)S(1)}, /*index=5*/s32[]{:T(128)}) %tuple.90), condition=%wide.region_5.7_spmd, body=%wide.region_4.6_spmd.sunk | while | flops 448578 | bytes 2977493 | solution.py:36
  249.7 2.2 gather_fusion.1
  257.7 2.2 gather_fusion.1
  265.8 2.2 gather_fusion.1
  277.8 2.2 gather_fusion.1
  285.9 2.2 gather_fusion.1
  293.9 2.2 gather_fusion.1
  305.9 2.2 gather_fusion.1
  314.0 2.2 gather_fusion.1
  322.0 2.2 gather_fusion.1
  326.0 2.2 gather_fusion.1
  334.1 2.2 gather_fusion.1
  342.1 2.2 gather_fusion.1
  354.2 2.2 gather_fusion.1
  362.2 2.2 gather_fusion.1
  370.9 2.4 collective-permute-start.4
  375.5 2.8 collective-permute-done.5
  378.3 7.2 collective-permute-done.4
  386.7 120.5 %while.41 = (s32[]{:T(128)}, f32[576,256]{1,0:T(8,128)S(1)}, f32[576,30]{0,1:T(8,128)}, s32[576,30]{0,1:T(8,128)}, f32[1728,256]{1,0:T(8,128)S(1)}, /*index=5*/s32[]{:T(128)}) while((s32[]{:T(128)}, f32[576,256]{1,0:T(8,128)S(1)}, f32[576,30]{0,1:T(8,128)}, s32[576,30]{0,1:T(8,128)}, f32[1728,256]{1,0:T(8,128)S(1)}, /*index=5*/s32[]{:T(128)}) %tuple.93), condition=%wide.region_7.9_spmd, body=%wide.region_6.8_spmd.sunk | while | flops 448578 | bytes 2977493 | solution.py:36
  392.3 2.2 gather_fusion.2
  400.3 2.2 gather_fusion.2
  408.4 2.2 gather_fusion.2
  412.4 2.2 gather_fusion.2
  420.4 2.2 gather_fusion.2
  428.4 2.2 gather_fusion.2
  440.5 2.2 gather_fusion.2
  448.5 2.2 gather_fusion.2
  456.6 2.2 gather_fusion.2
  468.6 2.2 gather_fusion.2
  476.6 2.2 gather_fusion.2
  484.7 2.2 gather_fusion.2
  488.7 2.2 gather_fusion.2
  496.7 2.2 gather_fusion.2
  504.8 2.2 gather_fusion.2
  512.7 247.3 %all-reduce = (f32[1000,16]{0,1:T(8,128)}, f32[16]{0:T(128)S(1)}) all-reduce(f32[1000,16]{0,1:T(8,128)} %fusion.3, f32[16]{0:T(128)S(1)} %copy-done.9), channel_id=1, replica_groups=mesh['cell'=64,'gene'=8] {'cell'}, use_global_device_ids=true, to_apply=%region_11.13 | all-reduce | flops 16016 | bytes 128128 | tf_op jit(solution)/shard_map/psum | solution.py:94
  761.4 2.8 fusion.27
  767.5 246.9 %psum.39 = f32[1000,16]{0,1:T(8,128)} all-reduce(f32[1000,16]{0,1:T(8,128)S(1)} %fusion.18), channel_id=1, replica_groups=mesh['cell'=64,'gene'=8] {'cell'}, use_global_device_ids=true, to_apply=%region_19.21 | all-reduce | flops 16000 | bytes 128000 | tf_op jit(solution)/shard_map/psum | solution.py:96
  1015.9 2.4 broadcast_divide_fusion
  (637 shorter events, 283.3 us)
Async XLA Ops:
  7.2 1.3 copy-start
  7.2 89.0 %copy-start.4 = (f32[576,30]{0,1:T(8,128)S(1)}, f32[576,30]{0,1:T(8,128)}, u32[]{:S(2)}) copy-start(f32[576,30]{0,1:T(8,128)} %param.21) | copy-start | bytes 207364
  7.2 89.0 %copy-start.8 = (s32[576]{0:T(1024)S(1)}, s32[576]{0:T(1024)}, u32[]{:S(2)}) copy-start(s32[576]{0:T(1024)} %param.20) | copy-start | bytes 6916
  7.2 90.3 %copy-start.5 = (s32[576,30]{0,1:T(8,128)S(1)}, s32[576,30]{0,1:T(8,128)}, u32[]{:S(2)}) copy-start(s32[576,30]{0,1:T(8,128)} %param.19) | copy-start | bytes 207364
  7.2 84.7 %all-reduce.4.cloned.1.call-start = ((), (), s32[]{:S(2)}) async-start(), calls=%async_computation | async-start | bytes 1179648 | tf_op jit(solution)/shard_map/psum | solution.py:84
  10.6 1003.8 %all-reduce.6.cloned.1.call-start = ((), (), s32[]{:S(2)}) async-start(), calls=%async_computation.1 | async-start | bytes 2048000 | tf_op jit(solution)/shard_map/psum | solution.py:96
  91.9 9.6 collective-permute-start.1
  93.8 14.7 %collective-permute-start = (f32[576,256]{1,0:T(8,128)}, f32[576,256]{1,0:T(8,128)S(1)}, u32[]{:S(2)}, u32[]{:S(2)}) collective-permute-start(f32[576,256]{1,0:T(8,128)} %all-reduce.4.cloned.1.call-done), channel_id=1, source_target_pairs={{0,8},{8,16},{16,24},{24,32},{32,40},{40,48},{48,56},{56,64},{64,7... | collective-permute-start | bytes 1769480 | tf_op jit(solution)/shard_map/ppermute | solution.py:22
  96.9 0.6 copy-start.7
  98.1 11.6 %copy-start.1 = (f32[576,256]{1,0:T(8,128)S(1)}, f32[576,256]{1,0:T(8,128)}, u32[]{:S(2)}) copy-start(f32[576,256]{1,0:T(8,128)} %all-reduce.4.cloned.1.call-done) | copy-start | bytes 1769476
  230.4 9.3 collective-permute-start.3
  232.3 14.6 %collective-permute-start.2 = (f32[576,256]{1,0:T(8,128)S(1)}, f32[576,256]{1,0:T(8,128)}, u32[]{:S(2)}, u32[]{:S(2)}) collective-permute-start(f32[576,256]{1,0:T(8,128)S(1)} %broadcast_divide_fusion.3), channel_id=1, source_target_pairs={{0,8},{8,16},{16,24},{24,32},{32,40},{40,48},{48,56},{56,64},{64,7... | collective-permute-start | bytes 1769480 | tf_op jit(solution)/shard_map/ppermute | solution.py:22
  368.7 6.0 copy-start.3
  368.8 9.4 collective-permute-start.5
  370.9 14.6 %collective-permute-start.4 = (f32[576,256]{1,0:T(8,128)S(1)}, f32[576,256]{1,0:T(8,128)}, u32[]{:S(2)}, u32[]{:S(2)}) collective-permute-start(f32[576,256]{1,0:T(8,128)S(1)} %broadcast_divide_fusion.2), channel_id=1, source_target_pairs={{0,8},{8,16},{16,24},{24,32},{32,40},{40,48},{48,56},{56,64},{64,7... | collective-permute-start | bytes 1769480 | tf_op jit(solution)/shard_map/ppermute | solution.py:22
  508.9 2.1 copy-start.6
  511.0 1.7 copy-start.9
  764.6 1.7 copy-start.2
Sparse Core Ops, SparseCore 0:
  11.0 80.8 all-reduce.3
  766.5 189.0 all-reduce.5
where the time goes:
time: 1040 us; the launch traced here: 1030 us
  blocking collectives  494 us (48%)
  local copies, waits for them, and re-layouts  331 us (32%)
  waiting for transfers between devices  114 us (11%)
  other arithmetic  41.5 us (4%)
  between operations  14.3 us (1%)
  starting transfers between devices  13.2 us (1%)
  matrix products  11.8 us (1%)
    psum x1, blocking collectives, shards(): first_obs, batch_sizes = lax.psum((first_obs, batch_sizes), 'cell')  247 us
    psum x1, blocking collectives, shards(): cent_sums, final_obs = lax.psum((cent_sums, final_obs), 'cell')  247 us
    gather x90, local copies, waits for them, and re-layouts, add_slot(): return total_sum + weight * jnp.take(padded, column, axis=0)  195 us
    psum x1, waiting for transfers between devices, shards(): state_field = lax.psum(partial_value, 'gene')  81.2 us
    dynamic_slice x90, local copies, waits for them, and re-layouts, add_slot(): weight = lax.dynamic_slice_in_dim(weights, slot, 1, 1)  67.4 us
    dynamic_slice x90, local copies, waits for them, and re-layouts, add_slot(): column = lax.dynamic_slice_in_dim(local_index, slot, 1, 1)[:, 0]  67.2 us
    add x90, other arithmetic, add_slot(): return total_sum + weight * jnp.take(padded, column, axis=0)  25.3 us
    ppermute x3, waiting for transfers between devices, with_halo(): before = lax.ppermute(last, axis, up)  21.5 us
  transfers between devices with their start and end apart: 8, of which 7 were waited for; matrix products, arithmetic and copies ran while one was open for 0% of the time, Pallas kernels for 0%

commit v1 on v0

v1 whole, which is shorter than its diff:
```python
import functools

import jax
import jax.numpy as jnp
from jax import lax
from jax.experimental import pallas as pl
from jax.experimental.pallas import tpu as pltpu
from jax.sharding import PartitionSpec as P

B = 16
NBR = 30
DIFF_STEPS = 3
EPSILON = 1e-06
SIGMA_SCALE = 0.1
LANE = 128
MESH = pl.DeviceIdType.MESH
BF16 = jnp.bfloat16
F32 = jnp.float32


def padded(size, unit=LANE):
    return -(-size // unit) * unit


def split2(x):
    hi = x.astype(BF16)
    return hi, (x - hi.astype(F32)).astype(BF16)


def split3(x):
    hi = x.astype(BF16)
    rest = x - hi.astype(F32)
    mid = rest.astype(BF16)
    return hi, mid, (rest - mid.astype(F32)).astype(BF16)


def dot(a, b):
    return jnp.dot(a, b, preferred_element_type=F32)


def dot_nt(a, b):
    return lax.dot_general(a, b, (((1,), (1,)), ((), ())), preferred_element_type=F32)


def dot_tn(a, b):
    return lax.dot_general(a, b, (((0,), (0,)), ((), ())), preferred_element_type=F32)


def weights_kernel(rows, index_ref, weight_ref, hi_ref, lo_ref):
    wide = hi_ref.shape[1]
    hi_ref[...] = jnp.zeros_like(hi_ref)
    lo_ref[...] = jnp.zeros_like(lo_ref)
    tile = LANE
    for at in range(wide // tile):
        lanes = slice(at * tile, (at + 1) * tile)
        spans = ((0, at, wide // tile), (1, 0, wide // tile), (2, 0, at + 1))
        for block, first, last in spans:

            def fill(step, carry, block=block, lanes=lanes):
                start = pl.multiple_of(step * tile, tile)
                source = lax.broadcasted_iota(jnp.int32, (tile, tile), 0) + (
                    start + (block - 1) * rows
                )
                total = jnp.zeros((tile, tile), F32)
                for slot in range(NBR):
                    hit = index_ref[slot : slot + 1, lanes] == source
                    total += jnp.where(hit, weight_ref[slot : slot + 1, lanes], 0.0)
                inside = source < block * rows
                total = jnp.where(inside, total, 0.0)
                hi, lo = split2(total)
                hi_ref[pl.ds(block * wide + start, tile), lanes] = hi
                lo_ref[pl.ds(block * wide + start, tile), lanes] = lo
                return carry

            lax.fori_loop(first, last, fill, 0)


def main_kernel(
    dims,
    part_ref,
    w_hi,
    w_lo,
    inverse_ref,
    batch_ref,
    cent_ref,
    smooth_ref,
    new_cent_ref,
    obs_ref,
    rs_slots,
    state,
    halo,
    full,
    unit,
    k_hi,
    k_lo,
    fo_own,
    fo_in,
    fo_mid,
    fo_out,
    fo_all,
    pen3,
    cs,
    cs_in,
    cs_mid,
    cs_out,
    cs_end,
    fb_own,
    fb_in,
    fb_mid,
    fb_out,
    y_send,
    y_recv,
    h_send,
    h_recv,
    a_send,
    a_recv,
    c_send,
    c_recv,
):
    rows, k_real, n_gene, n_in, n_out = dims
    n_cell = n_in * n_out
    comps, wide = part_ref.shape
    share = comps // n_gene
    chunk = cent_ref.shape[0] // n_gene
    piece = chunk // n_in
    half = chunk // 2
    cell = lax.axis_index("cell")
    gene = lax.axis_index("gene")
    inner = lax.rem(cell, n_in)
    outer = lax.div(cell, n_in)
    core = lax.rem(cell, 2)

    def along_y(d):
        return (cell, lax.rem(gene + d, n_gene))

    def along_in(d):
        return (outer * n_in + lax.rem(inner + d, n_in), gene)

    def along_out(d):
        return (lax.rem(outer + d, n_out) * n_in + inner, gene)

    after = (lax.rem(cell + 1, n_cell), gene)
    before = (lax.rem(cell + n_cell - 1, n_cell), gene)
    twin = (cell + 1 - 2 * core, gene)

    barrier = pltpu.get_barrier_semaphore()
    greeted = (
        [along_y(d) for d in range(1, n_gene)]
        + [along_in(d) for d in range(1, n_in)]
        + [along_out(d) for d in range(1, n_out)]
        + [after, before]
    )
    for target in greeted:
        pl.semaphore_signal(barrier, inc=1, device_id=target, device_id_type=MESH)
    pl.semaphore_wait(barrier, len(greeted))

    pending = []

    def send(src, dst, send_sem, recv_sem, target):
        copy = pltpu.make_async_remote_copy(
            src_ref=src,
            dst_ref=dst,
            send_sem=send_sem,
            recv_sem=recv_sem,
            device_id=target,
            device_id_type=MESH,
        )
        copy.start()
        pending.append(copy)
        return copy

    copies = []
    for d in range(1, n_gene):
        to = lax.rem(gene + d, n_gene)
        copies.append(
            send(
                part_ref.at[pl.ds(pl.multiple_of(to * share, share), share)],
                rs_slots.at[d - 1],
                y_send.at[0, d - 1],
                y_recv.at[0, d - 1],
                along_y(d),
            )
        )
    own = pl.ds(pl.multiple_of(gene * share, share), share)
    value = part_ref[own, :]
    for d in range(1, n_gene):
        copies[d - 1].wait_recv()
        value += rs_slots[d - 1]

    def spread(field, block):
        hi, lo = split2(field)
        span = slice(block * wide, (block + 1) * wide)
        both = dot(jnp.concatenate([hi, lo], axis=0), w_hi[span, :])
        return both[:share] + both[share:] + dot(hi, w_lo[span, :])

    for step in range(DIFF_STEPS):
        state[step] = value
        up = send(
            state.at[step], halo.at[step, 0], h_send.at[step, 0], h_recv.at[step, 0], after
        )
        down = send(
            state.at[step], halo.at[step, 1], h_send.at[step, 1], h_recv.at[step, 1], before
        )
        total = value + spread(value, 1)
        up.wait_recv()
        total += spread(halo[step, 0], 0)
        down.wait_recv()
        total += spread(halo[step, 1], 2)
        value = total * inverse_ref[0:1, :]

    full[own, :] = value
    copies = []
    for d in range(1, n_gene):
        copies.append(
            send(full.at[own], full.at[own], y_send.at[1, d - 1], y_recv.at[1, d - 1], along_y(d))
        )
    smooth_ref[...] = value[:, :rows]
    onehot = (
        batch_ref[0:1, :] == lax.broadcasted_iota(jnp.int32, (B, wide), 0)
    ).astype(F32)
    counts = jnp.sum(onehot, axis=1, keepdims=True)
    hot = onehot.astype(BF16)
    for copy in copies:
        copy.wait_recv()

    whole = full[...]
    norm = jnp.sqrt(jnp.sum(whole * whole, axis=0, keepdims=True) + EPSILON)
    unit[...] = (whole / norm).astype(BF16)

    def kernel_rows(start):
        scores = dot(cent_ref[pl.ds(start, chunk), :], unit[...])
        number = lax.broadcasted_iota(jnp.int32, (chunk, wide), 0) + start
        return jnp.where(number < k_real, jnp.exp((scores - 1.0) * (2.0 / SIGMA_SCALE)), 0.0)

    def first(at, sums):
        start = pl.multiple_of(at * chunk, chunk)
        values = kernel_rows(start)
        hi, lo = split2(values)
        k_hi[pl.ds(start, chunk), :] = hi
        k_lo[pl.ds(start, chunk), :] = lo
        return sums + jnp.sum(values, axis=0, keepdims=True)

    sums = lax.fori_loop(0, n_gene, first, jnp.zeros((1, wide), F32))
    mine = pl.multiple_of(gene * chunk, chunk)
    kernel_own = kernel_rows(mine)
    hi, lo = split2(kernel_own / sums)
    observed = dot_nt(hot, hi) + dot_nt(hot, lo)
    column = lax.broadcasted_iota(jnp.int32, (B, chunk), 1) + gene * chunk
    fo_own[...] = jnp.where(column == n_gene * chunk - 1, counts, observed)

    def all_sum(source, slots, target_of, count, sems, at):
        send_sem, recv_sem = sems
        copies = []
        for d in range(1, count):
            copies.append(
                send(
                    source,
                    slots.at[d - 1],
                    send_sem.at[at, d - 1],
                    recv_sem.at[at, d - 1],
                    target_of(d),
                )
            )

        def finish():
            total = source[...]
            for d in range(1, count):
                copies[d - 1].wait_recv()
                total += slots[d - 1]
            return total

        return finish

    a_sems = (a_send, a_recv)
    fo_mid[...] = all_sum(fo_own, fo_in, along_in, n_in, a_sems, 0)()
    fo_all[gene] = all_sum(fo_mid, fo_out, along_out, n_out, a_sems, 1)()
    copies = []
    for d in range(1, n_gene):
        copies.append(
            send(
                fo_all.at[gene],
                fo_all.at[gene],
                y_send.at[2, d - 1],
                y_recv.at[2, d - 1],
                along_y(d),
            )
        )
    for copy in copies:
        copy.wait_recv()

    sizes = fo_all[n_gene - 1][:, chunk - 1 : chunk]
    portion = sizes / jnp.sum(sizes, axis=0, keepdims=True)

    def penalty_of(seen):
        ratio = (jnp.sum(seen, axis=0, keepdims=True) * portion + 1.0) / (seen + 1.0)
        return jnp.concatenate(split3(ratio * ratio), axis=0)

    for at in range(n_gene):
        pen3[:, at * chunk : (at + 1) * chunk] = penalty_of(fo_all[at])
    parts = dot(pen3[...], k_hi[...]) + dot(pen3[...], k_lo[...])
    parts = (parts[:B] + parts[B : 2 * B]) + parts[2 * B :]
    weighted = jnp.sum(parts * onehot, axis=0, keepdims=True)
    lane = lax.broadcasted_iota(jnp.int32, (1, wide), 1)
    weighted = jnp.where(lane < rows, weighted, 1.0)
    factor = dot_tn(penalty_of(fo_all[gene]), jnp.concatenate([hot, hot, hot], axis=0))
    response = (kernel_own * factor / weighted).astype(BF16)
    cs[...] = dot_nt(response, unit[...])
    fb_own[...] = dot_nt(hot, response)

    c_copies = []
    for d in range(1, n_in):
        to = lax.rem(inner + d, n_in)
        c_copies.append(
            send(
                cs.at[pl.ds(pl.multiple_of(to * piece, piece), piece)],
                cs_in.at[d - 1],
                c_send.at[0, d - 1],
                c_recv.at[0, d - 1],
                along_in(d),
            )
        )
    fb_first = all_sum(fb_own, fb_in, along_in, n_in, a_sems, 2)
    piece_sum = cs[pl.ds(pl.multiple_of(inner * piece, piece), piece), :]
    for d in range(1, n_in):
        c_copies[d - 1].wait_recv()
        piece_sum += cs_in[d - 1]
    cs_mid[...] = piece_sum
    cs_second = all_sum(cs_mid, cs_out, along_out, n_out, (c_send, c_recv), 1)
    fb_mid[...] = fb_first()
    fb_second = all_sum(fb_mid, fb_out, along_out, n_out, a_sems, 3)
    piece_sum = cs_second()
    length = jnp.sqrt(jnp.sum(piece_sum * piece_sum, axis=1, keepdims=True) + EPSILON)
    cs_end[...] = piece_sum / length

    here = pl.ds(pl.multiple_of(gene * chunk + inner * piece, piece), piece)
    copies = []
    for d in range(1, n_in):
        copies.append(
            send(
                cs_end,
                new_cent_ref.at[here],
                c_send.at[2, d - 1],
                c_recv.at[2, d - 1],
                along_in(d),
            )
        )
    new_cent_ref[here, :] = cs_end[...]
    obs_ref[gene] = fb_second()
    obs_copies = []
    for d in range(1, n_gene):
        obs_copies.append(
            send(
                obs_ref.at[gene],
                obs_ref.at[gene],
                y_send.at[3, d - 1],
                y_recv.at[3, d - 1],
                along_y(d),
            )
        )
    for copy in copies:
        copy.wait_recv()

    def half_of(number):
        return pl.ds(pl.multiple_of(number * chunk + core * half, half), half)

    copies = []
    for d in range(1, n_gene):
        copies.append(
            send(
                new_cent_ref.at[half_of(gene)],
                new_cent_ref.at[half_of(gene)],
                y_send.at[4, d - 1],
                y_recv.at[4, d - 1],
                along_y(d),
            )
        )
    shared = []
    for d in range(1, n_gene):
        copies[d - 1].wait_recv()
        rows_at = half_of(lax.rem(gene + n_gene - d, n_gene))
        shared.append(
            send(
                new_cent_ref.at[rows_at],
                new_cent_ref.at[rows_at],
                y_send.at[5, d - 1],
                y_recv.at[5, d - 1],
                twin,
            )
        )
    for copy in obs_copies:
        copy.wait_recv()
    for copy in shared:
        copy.wait_recv()
    for copy in pending:
        copy.wait_send()


def shards(n_in, expression, gene_mean, loadings, nbr_index, nbr_count, nbr_weight, batch, centroids):
    rows = expression.shape[0]
    comps = loadings.shape[1]
    k_real = centroids.shape[0]
    n_gene = lax.axis_size("gene")
    n_out = lax.axis_size("cell") // n_in
    wide = padded(rows)
    k_wide = padded(k_real)
    share = comps // n_gene
    chunk = k_wide // n_gene
    piece = chunk // n_in
    lanes = ((0, 0), (0, wide - rows))

    mean_proj = jnp.dot(gene_mean, loadings.astype(F32), precision=lax.Precision.HIGHEST)
    partial = lax.dot_general(
        loadings, expression, (((0,), (1,)), ((), ())), preferred_element_type=F32
    )
    partial = jnp.pad(partial - mean_proj[:, None], lanes)

    live = jnp.arange(NBR)[:, None] < nbr_count[None, :]
    weights = jnp.where(live, nbr_weight.T, jnp.float32(0.0))
    inverse = 1.0 / (1.0 + jnp.sum(weights, axis=0, keepdims=True))
    inverse = jnp.pad(jnp.broadcast_to(inverse, (8, rows)), lanes)
    local = nbr_index.T - lax.axis_index("cell") * rows
    slots = ((0, 32 - NBR), (0, wide - rows))
    local = jnp.pad(local, slots)
    weights = jnp.pad(weights, slots)
    batch_row = jnp.pad(jnp.broadcast_to(batch[None, :], (8, rows)), lanes, constant_values=-1)
    cent_norm = jnp.sqrt(jnp.sum(centroids * centroids, axis=1, keepdims=True) + EPSILON)
    cent_unit = jnp.pad((centroids / cent_norm).astype(BF16), ((0, k_wide - k_real), (0, 0)))

    vmem = pl.BlockSpec(memory_space=pltpu.VMEM)
    w_hi, w_lo = pl.pallas_call(
        functools.partial(weights_kernel, rows),
        out_shape=[jax.ShapeDtypeStruct((3 * wide, wide), BF16)] * 2,
        in_specs=[vmem] * 2,
        out_specs=[vmem] * 2,
        compiler_params=pltpu.CompilerParams(vmem_limit_bytes=32 * 1024 * 1024),
    )(local, weights)

    dims = (rows, k_real, n_gene, n_in, n_out)
    dma = pltpu.SemaphoreType.DMA
    smooth, new_cent, obs = pl.pallas_call(
        functools.partial(main_kernel, dims),
        out_shape=[
            jax.ShapeDtypeStruct((share, rows), F32),
            jax.ShapeDtypeStruct((k_wide, comps), F32),
            jax.ShapeDtypeStruct((n_gene, B, chunk), F32),
        ],
        in_specs=[vmem] * 6,
        out_specs=[vmem] * 3,
        scratch_shapes=[
            pltpu.VMEM((n_gene - 1, share, wide), F32),
            pltpu.VMEM((DIFF_STEPS, share, wide), F32),
            pltpu.VMEM((DIFF_STEPS, 2, share, wide), F32),
            pltpu.VMEM((comps, wide), F32),
            pltpu.VMEM((comps, wide), BF16),
            pltpu.VMEM((k_wide, wide), BF16),
            pltpu.VMEM((k_wide, wide), BF16),
            pltpu.VMEM((B, chunk), F32),
            pltpu.VMEM((n_in - 1, B, chunk), F32),
            pltpu.VMEM((B, chunk), F32),
            pltpu.VMEM((n_out - 1, B, chunk), F32),
            pltpu.VMEM((n_gene, B, chunk), F32),
            pltpu.VMEM((3 * B, k_wide), BF16),
            pltpu.VMEM((chunk, comps), F32),
            pltpu.VMEM((n_in - 1, piece, comps), F32),
            pltpu.VMEM((piece, comps), F32),
            pltpu.VMEM((n_out - 1, piece, comps), F32),
            pltpu.VMEM((piece, comps), F32),
            pltpu.VMEM((B, chunk), F32),
            pltpu.VMEM((n_in - 1, B, chunk), F32),
            pltpu.VMEM((B, chunk), F32),
            pltpu.VMEM((n_out - 1, B, chunk), F32),
            dma((6, n_gene - 1)),
            dma((6, n_gene - 1)),
            dma((DIFF_STEPS, 2)),
            dma((DIFF_STEPS, 2)),
            dma((4, max(n_in, n_out) - 1)),
            dma((4, max(n_in, n_out) - 1)),
            dma((3, max(n_in, n_out) - 1)),
            dma((3, max(n_in, n_out) - 1)),
        ],
        compiler_params=pltpu.CompilerParams(
            collective_id=0, has_side_effects=True, vmem_limit_bytes=48 * 1024 * 1024
        ),
    )(partial, w_hi, w_lo, inverse, batch_row, cent_unit)

    final_obs = obs.transpose(0, 2, 1).reshape(k_wide, B)[:k_real]
    return (smooth.T, new_cent[:k_real], final_obs)


def solution(mesh):
    in_specs = (
        P("cell", "gene"),
        P("gene"),
        P("gene", None),
        P("cell", None),
        P("cell"),
        P("cell", None),
        P("cell"),
        P(),
    )
    out_specs = (P("cell", "gene"), P(), P())
    n_in = 8 if mesh.shape["cell"] % 64 == 0 else 2
    body = functools.partial(shards, n_in)
    return jax.shard_map(body, mesh=mesh, in_specs=in_specs, out_specs=out_specs, check_vma=False)
```

time: 1040 us -> 134 us (0.13)
  the two profiles are of different devices: /device:TPU:256 before, /device:TPU:1 now
where the time goes in v1:
time: 134 us
  Pallas kernels  123 us (92%)
  local copies, waits for them, and re-layouts  4.59 us (3%)
  other arithmetic  3.45 us (3%)
  matrix products  1.68 us (1%)
    pallas_call x1, Pallas kernels, shards(): pl.pallas_call(functools.partial(main_kernel, dims), out_shape=[jax.Shape...  111 us
    pallas_call x1, Pallas kernels, shards(): pl.pallas_call(functools.partial(weights_kernel, rows), out_shape=[jax.Sh...  12.3 us

profile of v1, /device:TPU:1, one launch (start us, length us, event | category | flops | bytes accessed | tf_op | source)
XLA Modules:
  0.0 133.6 jit_solution(8578640114723133877)
XLA Ops:
  0.6 0.0 copy-start
  0.6 0.0 copy-start.2
  0.7 0.0 copy-start.3
  0.7 1.3 fusion.1
  1.9 0.7 pad.33
  2.7 1.4 %multiply_reduce_fusion = f32[1000]{0:T(1024)S(1)} fusion(f32[1000,256]{1,0:T(8,128)} %param.15), kind=kLoop, calls=%fused_computation.2 | loop fusion | flops 511000 | bytes 1028000 | tf_op jit(solution)/shard_map/reduce_sum | solution.py:426
  4.1 0.9 subtract_bitcast_fusion
  5.0 0.9 fusion
  6.0 0.0 copy-done.2
  6.0 0.2 divide_convert_fusion
  6.3 0.0 copy-done
  6.3 0.0 copy-done.3
  6.3 0.4 convolution_subtract_fusion
  6.8 12.3 %shard_map.103 = (bf16[1920,640]{1,0:T(8,128)(2,1)S(1)}, bf16[1920,640]{1,0:T(8,128)(2,1)S(1)}) custom-call(s32[32,640]{1,0:T(8,128)S(1)} %pad.29.index_ref, f32[32,640]{1,0:T(8,128)S(1)} %pad.30.weight_ref), custom_call_target="tpu_custom_call" | custom-call | tf_op jit(solution)/shard_map/pallas_call | solution.py:430
  19.1 0.0 copy-start.1
  19.1 1.4 %copy-done.1 = bf16[1920,640]{1,0:T(8,128)(2,1)} copy-done((bf16[1920,640]{1,0:T(8,128)(2,1)}, bf16[1920,640]{1,0:T(8,128)(2,1)S(1)}, u32[]{:S(2)}) %copy-start.1) | copy-done | bytes 2457624
  20.5 110.7 %shard_map.104 = (f32[32,576]{1,0:T(8,128)S(1)}, f32[1024,256]{1,0:T(8,128)S(1)}, f32[8,16,128]{2,1,0:T(8,128)S(1)}) custom-call(f32[256,640]{1,0:T(8,128)S(1)} %pad.28.part_ref, bf16[1920,640]{1,0:T(8,128)(2,1)S(1)} %get-tuple-element.8.w_hi, bf16[1920,640]{1,0:T(8,128)(2,1)} %copy-done.1, f32[8,640]{1,0:T(8,128)S(1)} %pad.32.inverse_ref, ...), custom_call_target="tpu_custom_call" | custom-call | tf_op jit(solution)/shard_map/pallas_call | solution.py:440
  131.3 0.6 copy_bitcast_fusion
  131.9 1.0 slice.6
  132.9 0.6 copy.21
  (9 shorter events, 0.1 us)
Async XLA Ops:
  0.6 5.7 %copy-start = (bf16[576,512]{1,0:T(8,128)(2,1)S(1)}, bf16[576,512]{1,0:T(8,128)(2,1)}, u32[]{:S(2)}) copy-start(bf16[576,512]{1,0:T(8,128)(2,1)} %param.8) | copy-start | bytes 1769476
  0.6 5.4 %copy-start.2 = (f32[1000,256]{1,0:T(8,128)S(1)}, f32[1000,256]{1,0:T(8,128)}, u32[]{:S(2)}) copy-start(f32[1000,256]{1,0:T(8,128)} %param.15) | copy-start | bytes 3072004
  0.7 5.6 %copy-start.3 = (bf16[512,256]{1,0:T(8,128)(2,1)S(1)}, bf16[512,256]{1,0:T(8,128)(2,1)}, u32[]{:S(2)}) copy-start(bf16[512,256]{1,0:T(8,128)(2,1)} %param.10) | copy-start | bytes 786436
  19.1 1.4 %copy-start.1 = (bf16[1920,640]{1,0:T(8,128)(2,1)}, bf16[1920,640]{1,0:T(8,128)(2,1)S(1)}, u32[]{:S(2)}) copy-start(bf16[1920,640]{1,0:T(8,128)(2,1)S(1)} %get-tuple-element.9.w_lo) | copy-start | bytes 7372804

commit v2 on v1

--- a/solution.py
+++ b/solution.py
@@ -46,7 +46,11 @@
     return lax.dot_general(a, b, (((0,), (0,)), ((), ())), preferred_element_type=F32)
 
 
-def weights_kernel(rows, index_ref, weight_ref, hi_ref, lo_ref):
+def farthest_first(count):
+    return sorted(range(1, count), key=lambda d: -min(d, count - d))
+
+
+def build_weights(rows, index_ref, weight_ref, hi_ref, lo_ref):
     wide = hi_ref.shape[1]
     hi_ref[...] = jnp.zeros_like(hi_ref)
     lo_ref[...] = jnp.zeros_like(lo_ref)
@@ -65,8 +69,7 @@
                 for slot in range(NBR):
                     hit = index_ref[slot : slot + 1, lanes] == source
                     total += jnp.where(hit, weight_ref[slot : slot + 1, lanes], 0.0)
-                inside = source < block * rows
-                total = jnp.where(inside, total, 0.0)
+                total = jnp.where(source < block * rows, total, 0.0)
                 hi, lo = split2(total)
                 hi_ref[pl.ds(block * wide + start, tile), lanes] = hi
                 lo_ref[pl.ds(block * wide + start, tile), lanes] = lo
@@ -77,15 +80,31 @@
 
 def main_kernel(
     dims,
+    expr_hbm,
+    mean_ref,
+    load_hbm,
+    index_hbm,
+    count_ref,
+    weight_hbm,
+    batch_ref,
+    centroid_hbm,
+    smooth_ref,
+    cent_out,
+    obs_out,
+    new_cent_ref,
+    obs_ref,
+    expr_ref,
+    load_ref,
+    index_ref,
+    weight_ref,
+    centroid_ref,
+    l_sem,
     part_ref,
+    idx,
+    wgt,
     w_hi,
     w_lo,
-    inverse_ref,
-    batch_ref,
     cent_ref,
-    smooth_ref,
-    new_cent_ref,
-    obs_ref,
     rs_slots,
     state,
     halo,
@@ -103,7 +122,6 @@
     cs_in,
     cs_mid,
     cs_out,
-    cs_end,
     fb_own,
     fb_in,
     fb_mid,
@@ -116,14 +134,17 @@
     a_recv,
     c_send,
     c_recv,
+    t_send,
+    t_recv,
 ):
     rows, k_real, n_gene, n_in, n_out = dims
     n_cell = n_in * n_out
     comps, wide = part_ref.shape
+    y_order, in_order = farthest_first(n_gene), farthest_first(n_in)
     share = comps // n_gene
     chunk = cent_ref.shape[0] // n_gene
     piece = chunk // n_in
-    half = chunk // 2
+    n_x = n_in // 2
     cell = lax.axis_index("cell")
     gene = lax.axis_index("gene")
     inner = lax.rem(cell, n_in)
@@ -142,6 +163,21 @@
     after = (lax.rem(cell + 1, n_cell), gene)
     before = (lax.rem(cell + n_cell - 1, n_cell), gene)
     twin = (cell + 1 - 2 * core, gene)
+
+    brought = [
+        pltpu.make_async_copy(source, target, l_sem.at[at])
+        for at, (source, target) in enumerate(
+            (
+                (load_hbm, load_ref),
+                (expr_hbm, expr_ref),
+                (index_hbm, index_ref),
+                (weight_hbm, weight_ref),
+                (centroid_hbm, centroid_ref),
+            )
+        )
+    ]
+    for copy in brought:
+        copy.start()
 
     barrier = pltpu.get_barrier_semaphore()
     greeted = (
@@ -152,6 +188,17 @@
     )
     for target in greeted:
         pl.semaphore_signal(barrier, inc=1, device_id=target, device_id_type=MESH)
+
+    mean = jnp.concatenate(
+        [m.astype(F32) for m in split3(mean_ref[...][None, :])] + [jnp.zeros((5, mean_ref.shape[0]), F32)],
+        axis=0,
+    ).astype(BF16)
+    brought[0].wait()
+    turned = load_ref[...].T
+    offset = jnp.sum(dot_nt(turned, mean), axis=1, keepdims=True)
+    brought[1].wait()
+    part_ref[:, rows:] = jnp.zeros((comps, wide - rows), F32)
+    part_ref[:, :rows] = dot_nt(turned, expr_ref[...]) - offset
     pl.semaphore_wait(barrier, len(greeted))
 
     pending = []
@@ -170,7 +217,7 @@
         return copy
 
     copies = []
-    for d in range(1, n_gene):
+    for d in y_order:
         to = lax.rem(gene + d, n_gene)
         copies.append(
             send(
@@ -182,9 +229,36 @@
             )
         )
     own = pl.ds(pl.multiple_of(gene * share, share), share)
+
+    brought[2].wait()
+    brought[3].wait()
+    idx[...] = jnp.full(idx.shape, -(4 * rows), jnp.int32)
+    idx[:NBR, :rows] = index_ref[...] - cell * rows
+    live = lax.broadcasted_iota(jnp.int32, (NBR, rows), 0) < count_ref[...][None, :]
+    kept = jnp.where(live, weight_ref[...], 0.0)
+    wgt[...] = jnp.zeros_like(wgt)
+    wgt[:NBR, :rows] = kept
+    build_weights(rows, idx, wgt, w_hi, w_lo)
+    inverse = 1.0 / (1.0 + jnp.sum(wgt[...], axis=0, keepdims=True))
+    brought[4].wait()
+    cents = centroid_ref[...]
+    cent_norm = jnp.sqrt(jnp.sum(cents * cents, axis=1, keepdims=True) + EPSILON)
+    cent_ref[...] = jnp.concatenate(
+        [cents / cent_norm, jnp.zeros((n_gene * chunk - k_real, comps), F32)], axis=0
+    ).astype(BF16)
+    onehot = jnp.concatenate(
+        [
+            (batch_ref[...][None, :] == lax.broadcasted_iota(jnp.int32, (B, rows), 0)).astype(F32),
+            jnp.zeros((B, wide - rows), F32),
+        ],
+        axis=1,
+    )
+    counts = jnp.sum(onehot, axis=1, keepdims=True)
+    hot = onehot.astype(BF16)
+
     value = part_ref[own, :]
-    for d in range(1, n_gene):
-        copies[d - 1].wait_recv()
+    for d, copy in zip(y_order, copies):
+        copy.wait_recv()
         value += rs_slots[d - 1]
 
     def spread(field, block):
@@ -206,20 +280,15 @@
         total += spread(halo[step, 0], 0)
         down.wait_recv()
         total += spread(halo[step, 1], 2)
-        value = total * inverse_ref[0:1, :]
+        value = total * inverse
 
     full[own, :] = value
     copies = []
-    for d in range(1, n_gene):
+    for d in y_order:
         copies.append(
             send(full.at[own], full.at[own], y_send.at[1, d - 1], y_recv.at[1, d - 1], along_y(d))
         )
     smooth_ref[...] = value[:, :rows]
-    onehot = (
-        batch_ref[0:1, :] == lax.broadcasted_iota(jnp.int32, (B, wide), 0)
-    ).astype(F32)
-    counts = jnp.sum(onehot, axis=1, keepdims=True)
-    hot = onehot.astype(BF16)
     for copy in copies:
         copy.wait_recv()
 
@@ -251,7 +320,7 @@
     def all_sum(source, slots, target_of, count, sems, at):
         send_sem, recv_sem = sems
         copies = []
-        for d in range(1, count):
+        for d in farthest_first(count):
             copies.append(
                 send(
                     source,
@@ -264,8 +333,8 @@
 
         def finish():
             total = source[...]
-            for d in range(1, count):
-                copies[d - 1].wait_recv()
+            for d, copy in zip(farthest_first(count), copies):
+                copy.wait_recv()
                 total += slots[d - 1]
             return total
 
@@ -275,7 +344,7 @@
     fo_mid[...] = all_sum(fo_own, fo_in, along_in, n_in, a_sems, 0)()
     fo_all[gene] = all_sum(fo_mid, fo_out, along_out, n_out, a_sems, 1)()
     copies = []
-    for d in range(1, n_gene):
+    for d in y_order:
         copies.append(
             send(
                 fo_all.at[gene],
@@ -308,7 +377,7 @@
     fb_own[...] = dot_nt(hot, response)
 
     c_copies = []
-    for d in range(1, n_in):
+    for d in in_order:
         to = lax.rem(inner + d, n_in)
         c_copies.append(
             send(
@@ -321,8 +390,8 @@
         )
     fb_first = all_sum(fb_own, fb_in, along_in, n_in, a_sems, 2)
     piece_sum = cs[pl.ds(pl.multiple_of(inner * piece, piece), piece), :]
-    for d in range(1, n_in):
-        c_copies[d - 1].wait_recv()
+    for d, copy in zip(in_order, c_copies):
+        copy.wait_recv()
         piece_sum += cs_in[d - 1]
     cs_mid[...] = piece_sum
     cs_second = all_sum(cs_mid, cs_out, along_out, n_out, (c_send, c_recv), 1)
@@ -330,24 +399,22 @@
     fb_second = all_sum(fb_mid, fb_out, along_out, n_out, a_sems, 3)
     piece_sum = cs_second()
     length = jnp.sqrt(jnp.sum(piece_sum * piece_sum, axis=1, keepdims=True) + EPSILON)
-    cs_end[...] = piece_sum / length
-
-    here = pl.ds(pl.multiple_of(gene * chunk + inner * piece, piece), piece)
+
+    new_cent_ref[gene, inner] = piece_sum / length
     copies = []
-    for d in range(1, n_in):
+    for d in y_order:
         copies.append(
             send(
-                cs_end,
-                new_cent_ref.at[here],
-                c_send.at[2, d - 1],
-                c_recv.at[2, d - 1],
-                along_in(d),
-            )
-        )
-    new_cent_ref[here, :] = cs_end[...]
+                new_cent_ref.at[gene, inner],
+                new_cent_ref.at[gene, inner],
+                y_send.at[4, d - 1],
+                y_recv.at[4, d - 1],
+                along_y(d),
+            )
+        )
     obs_ref[gene] = fb_second()
     obs_copies = []
-    for d in range(1, n_gene):
+    for d in y_order:
         obs_copies.append(
             send(
                 obs_ref.at[gene],
@@ -360,37 +427,36 @@
     for copy in copies:
         copy.wait_recv()
 
-    def half_of(number):
-        return pl.ds(pl.multiple_of(number * chunk + core * half, half), half)
-
-    copies = []
-    for d in range(1, n_gene):
-        copies.append(
-            send(
-                new_cent_ref.at[half_of(gene)],
-                new_cent_ref.at[half_of(gene)],
-                y_send.at[4, d - 1],
-                y_recv.at[4, d - 1],
-                along_y(d),
-            )
-        )
-    shared = []
-    for d in range(1, n_gene):
-        copies[d - 1].wait_recv()
-        rows_at = half_of(lax.rem(gene + n_gene - d, n_gene))
-        shared.append(
-            send(
-                new_cent_ref.at[rows_at],
-                new_cent_ref.at[rows_at],
-                y_send.at[5, d - 1],
-                y_recv.at[5, d - 1],
-                twin,
-            )
-        )
+    def column(number, target, sems, at):
+        send_sem, recv_sem = sems
+        return send(
+            new_cent_ref.at[:, number],
+            new_cent_ref.at[:, number],
+            send_sem.at[at],
+            recv_sem.at[at],
+            target,
+        )
+
+    x_order = farthest_first(n_x)
+    copies = [column(inner, along_in(2 * e), (c_send.at[2], c_recv.at[2]), e) for e in x_order]
+    shared = [column(inner, twin, (t_send, t_recv), 0)]
+    for e, copy in zip(x_order, copies):
+        copy.wait_recv()
+        number = lax.rem(inner + n_in - 2 * e, n_in)
+        shared.append(column(number, twin, (t_send, t_recv), e))
     for copy in obs_copies:
         copy.wait_recv()
+    for at in range(n_gene):
+        size = min(chunk, k_real - at * chunk)
+        obs_out[:, at * chunk : at * chunk + size] = obs_ref[at][:, :size]
     for copy in shared:
         copy.wait_recv()
+    for at in range(n_gene):
+        for part in range(n_in):
+            start = at * chunk + part * piece
+            size = min(piece, k_real - start)
+            if size > 0:
+                cent_out[start : start + size, :] = new_cent_ref[at, part][:size]
     for copy in pending:
         copy.wait_send()
 
@@ -406,47 +472,34 @@
     share = comps // n_gene
     chunk = k_wide // n_gene
     piece = chunk // n_in
-    lanes = ((0, 0), (0, wide - rows))
-
-    mean_proj = jnp.dot(gene_mean, loadings.astype(F32), precision=lax.Precision.HIGHEST)
-    partial = lax.dot_general(
-        loadings, expression, (((0,), (1,)), ((), ())), preferred_element_type=F32
-    )
-    partial = jnp.pad(partial - mean_proj[:, None], lanes)
-
-    live = jnp.arange(NBR)[:, None] < nbr_count[None, :]
-    weights = jnp.where(live, nbr_weight.T, jnp.float32(0.0))
-    inverse = 1.0 / (1.0 + jnp.sum(weights, axis=0, keepdims=True))
-    inverse = jnp.pad(jnp.broadcast_to(inverse, (8, rows)), lanes)
-    local = nbr_index.T - lax.axis_index("cell") * rows
-    slots = ((0, 32 - NBR), (0, wide - rows))
-    local = jnp.pad(local, slots)
-    weights = jnp.pad(weights, slots)
-    batch_row = jnp.pad(jnp.broadcast_to(batch[None, :], (8, rows)), lanes, constant_values=-1)
-    cent_norm = jnp.sqrt(jnp.sum(centroids * centroids, axis=1, keepdims=True) + EPSILON)
-    cent_unit = jnp.pad((centroids / cent_norm).astype(BF16), ((0, k_wide - k_real), (0, 0)))
-
     vmem = pl.BlockSpec(memory_space=pltpu.VMEM)
-    w_hi, w_lo = pl.pallas_call(
-        functools.partial(weights_kernel, rows),
-        out_shape=[jax.ShapeDtypeStruct((3 * wide, wide), BF16)] * 2,
-        in_specs=[vmem] * 2,
-        out_specs=[vmem] * 2,
-        compiler_params=pltpu.CompilerParams(vmem_limit_bytes=32 * 1024 * 1024),
-    )(local, weights)
-
+    hbm = pl.BlockSpec(memory_space=pltpu.HBM)
     dims = (rows, k_real, n_gene, n_in, n_out)
     dma = pltpu.SemaphoreType.DMA
     smooth, new_cent, obs = pl.pallas_call(
         functools.partial(main_kernel, dims),
         out_shape=[
             jax.ShapeDtypeStruct((share, rows), F32),
-            jax.ShapeDtypeStruct((k_wide, comps), F32),
-            jax.ShapeDtypeStruct((n_gene, B, chunk), F32),
+            jax.ShapeDtypeStruct((k_real, comps), F32),
+            jax.ShapeDtypeStruct((B, k_real), F32),
         ],
-        in_specs=[vmem] * 6,
+        in_specs=[hbm, vmem, hbm, hbm, vmem, hbm, vmem, hbm],
         out_specs=[vmem] * 3,
         scratch_shapes=[
+            pltpu.VMEM((n_gene, n_in, piece, comps), F32),
+            pltpu.VMEM((n_gene, B, chunk), F32),
+            pltpu.VMEM(expression.shape, BF16),
+            pltpu.VMEM(loadings.shape, BF16),
+            pltpu.VMEM((NBR, rows), jnp.int32),
+            pltpu.VMEM((NBR, rows), F32),
+            pltpu.VMEM(centroids.shape, F32),
+            dma((5,)),
+            pltpu.VMEM((comps, wide), F32),
+            pltpu.VMEM((32, wide), jnp.int32),
+            pltpu.VMEM((32, wide), F32),
+            pltpu.VMEM((3 * wide, wide), BF16),
+            pltpu.VMEM((3 * wide, wide), BF16),
+            pltpu.VMEM((k_wide, comps), BF16),
             pltpu.VMEM((n_gene - 1, share, wide), F32),
             pltpu.VMEM((DIFF_STEPS, share, wide), F32),
             pltpu.VMEM((DIFF_STEPS, 2, share, wide), F32),
@@ -464,7 +517,6 @@
             pltpu.VMEM((n_in - 1, piece, comps), F32),
             pltpu.VMEM((piece, comps), F32),
             pltpu.VMEM((n_out - 1, piece, comps), F32),
-            pltpu.VMEM((piece, comps), F32),
             pltpu.VMEM((B, chunk), F32),
             pltpu.VMEM((n_in - 1, B, chunk), F32),
             pltpu.VMEM((B, chunk), F32),
@@ -477,14 +529,24 @@
             dma((4, max(n_in, n_out) - 1)),
             dma((3, max(n_in, n_out) - 1)),
             dma((3, max(n_in, n_out) - 1)),
+            dma((n_in // 2,)),
+            dma((n_in // 2,)),
         ],
         compiler_params=pltpu.CompilerParams(
-            collective_id=0, has_side_effects=True, vmem_limit_bytes=48 * 1024 * 1024
+            collective_id=0, has_side_effects=True, vmem_limit_bytes=60 * 1024 * 1024
         ),
-    )(partial, w_hi, w_lo, inverse, batch_row, cent_unit)
-
-    final_obs = obs.transpose(0, 2, 1).reshape(k_wide, B)[:k_real]
-    return (smooth.T, new_cent[:k_real], final_obs)
+    )(
+        expression,
+        gene_mean,
+        loadings,
+        nbr_index.T,
+        nbr_count,
+        nbr_weight.T,
+        batch,
+        centroids,
+    )
+
+    return (smooth.T, new_cent, obs.T)
 
 
 def solution(mesh):
@@ -499,6 +561,6 @@
         P(),
     )
     out_specs = (P("cell", "gene"), P(), P())
-    n_in = 8 if mesh.shape["cell"] % 64 == 0 else 2
+    n_in = 8 if mesh.shape["cell"] % 64 == 0 else 4
     body = functools.partial(shards, n_in)
     return jax.shard_map(body, mesh=mesh, in_specs=in_specs, out_specs=out_specs, check_vma=False)

time: 134 us -> 109 us (0.81)
  Pallas kernels: 123 us -> 104 us
  other arithmetic: 3.45 us -> 0 us
  matrix products: 1.68 us -> 0 us
    pallas_call x1 -> x0, Pallas kernels: 12.3 us -> none  [shards(): pl.pallas_call(functools.partial(weights_kernel, rows), out_shape=[jax.Sh...]
    pallas_call x1, Pallas kernels: 111 us -> 104 us  [shards(): pl.pallas_call(functools.partial(main_kernel, dims), out_shape=[jax.Shape...]
    unnamed x9 -> x5, local copies, waits for them, and re-layouts: 2.08 us -> 4.43 us
    reduce_sum x2 -> x0, other arithmetic: 2.34 us -> none  [the longest x1 1.42 us: shards(): jnp.sum(centroids * centroids, axis=1, keepdims=True) + EPSILON]
    dot_general x2 -> x0, matrix products: 1.68 us -> none  [the longest x1 1.27 us: shards(): jnp.dot(gene_mean, loadings.astype(F32), precision=lax.Precision.HIGHEST)]
where the time goes in v2:
time: 109 us
  Pallas kernels  104 us (95%)
  local copies, waits for them, and re-layouts  4.43 us (4%)
    pallas_call x1, Pallas kernels, shards(): pl.pallas_call(functools.partial(main_kernel, dims), out_shape=[jax.Shape...  104 us
    unnamed x5, local copies, waits for them, and re-layouts  4.43 us

profile of v2, /device:TPU:1, one launch (start us, length us, event | category | flops | bytes accessed | tf_op | source)
XLA Modules:
  0.0 108.7 jit_solution(3805349958160289395)
XLA Ops:
  0.6 103.6 %shard_map.103 = (f32[32,576]{1,0:T(8,128)}, f32[1000,256]{1,0:T(8,128)}, f32[16,1000]{1,0:T(8,128)}) custom-call(bf16[576,512]{1,0:T(8,128)(2,1)} %expr_hbm.1, f32[512]{0:T(512)} %mean_ref.1, bf16[512,256]{1,0:T(8,128)(2,1)} %load_hbm.1, s32[30,576]{1,0:T(8,128)} %bitcast.4, s32[576]{0:T(1024)} %count_ref.1, f32[30,576]{1,0:T(8,128)} %bitcast.5, ...), custom_call_target="tpu_custom_call" | custom-call | tf_op jit(solution)/shard_map/pallas_call | solution.py:479
  104.2 1.5 %copy.14 = f32[576,32]{0,1:T(8,128)} copy(f32[576,32]{0,1:T(8,128)} %bitcast.6) | data formatting | bytes 147456
  105.8 0.0 copy-start
  105.8 2.3 %copy.15 = f32[1000,256]{1,0:T(8,128)} copy(f32[1000,256]{1,0:T(8,128)} %get-tuple-element.13) | data formatting | bytes 2048000
  108.0 0.0 copy-done
  108.0 0.6 copy.16
Async XLA Ops:
  105.8 2.3 %copy-start = (f32[16,1000]{1,0:T(8,128)S(1)}, f32[16,1000]{1,0:T(8,128)}, u32[]{:S(2)}) copy-start(f32[16,1000]{1,0:T(8,128)} %get-tuple-element.8) | copy-start | bytes 192004

commit v3 on v2

--- a/solution.py
+++ b/solution.py
@@ -50,32 +50,37 @@
     return sorted(range(1, count), key=lambda d: -min(d, count - d))
 
 
-def build_weights(rows, index_ref, weight_ref, hi_ref, lo_ref):
+def build_weights(rows, block, index_ref, weight_ref, hi_ref, lo_ref):
     wide = hi_ref.shape[1]
-    hi_ref[...] = jnp.zeros_like(hi_ref)
-    lo_ref[...] = jnp.zeros_like(lo_ref)
     tile = LANE
-    for at in range(wide // tile):
+    tiles = wide // tile
+    base = block * wide
+    span = slice(base, base + wide)
+    hi_ref[span, :] = jnp.zeros((wide, wide), BF16)
+    lo_ref[span, :] = jnp.zeros((wide, wide), BF16)
+    for at in range(tiles):
         lanes = slice(at * tile, (at + 1) * tile)
-        spans = ((0, at, wide // tile), (1, 0, wide // tile), (2, 0, at + 1))
-        for block, first, last in spans:
-
-            def fill(step, carry, block=block, lanes=lanes):
-                start = pl.multiple_of(step * tile, tile)
-                source = lax.broadcasted_iota(jnp.int32, (tile, tile), 0) + (
-                    start + (block - 1) * rows
-                )
-                total = jnp.zeros((tile, tile), F32)
-                for slot in range(NBR):
-                    hit = index_ref[slot : slot + 1, lanes] == source
-                    total += jnp.where(hit, weight_ref[slot : slot + 1, lanes], 0.0)
-                total = jnp.where(source < block * rows, total, 0.0)
-                hi, lo = split2(total)
-                hi_ref[pl.ds(block * wide + start, tile), lanes] = hi
-                lo_ref[pl.ds(block * wide + start, tile), lanes] = lo
-                return carry
-
-            lax.fori_loop(first, last, fill, 0)
+        first, last = ((at, tiles), (0, tiles), (0, at + 1))[block]
+
+        def rows_of(start, height, lanes=lanes):
+            source = lax.broadcasted_iota(jnp.int32, (height, tile), 0) + (
+                start + (block - 1) * rows
+            )
+            total = jnp.zeros((height, tile), F32)
+            for slot in range(NBR):
+                hit = index_ref[slot : slot + 1, lanes] == source
+                total += jnp.where(hit, weight_ref[slot : slot + 1, lanes], 0.0)
+            hi, lo = split2(total)
+            hi_ref[pl.ds(base + start, height), lanes] = hi
+            lo_ref[pl.ds(base + start, height), lanes] = lo
+
+        def fill(step, carry, rows_of=rows_of):
+            rows_of(pl.multiple_of(step * tile, tile), tile)
+            return carry
+
+        lax.fori_loop(first, min(last, rows // tile), fill, 0)
+        if last == tiles and rows % tile:
+            rows_of(rows // tile * tile, rows % tile)
 
 
 def main_kernel(
@@ -136,6 +141,12 @@
     c_recv,
     t_send,
     t_recv,
+    x_send,
+    x_recv,
+    o_sem,
+    turn,
+    smooth_v,
+    obs_v,
 ):
     rows, k_real, n_gene, n_in, n_out = dims
     n_cell = n_in * n_out
@@ -216,19 +227,34 @@
         pending.append(copy)
         return copy
 
-    copies = []
-    for d in y_order:
-        to = lax.rem(gene + d, n_gene)
-        copies.append(
-            send(
-                part_ref.at[pl.ds(pl.multiple_of(to * share, share), share)],
-                rs_slots.at[d - 1],
-                y_send.at[0, d - 1],
-                y_recv.at[0, d - 1],
-                along_y(d),
-            )
-        )
-    own = pl.ds(pl.multiple_of(gene * share, share), share)
+    half = share // 2
+    relay = n_gene == 8
+
+    def share_of(d, start=0, size=share):
+        at = lax.rem(gene + d, n_gene) * share + start
+        return pl.ds(pl.multiple_of(at, half), size)
+
+    own = share_of(0)
+    routes = (
+        (3, 0, share, 0, 1),
+        (5, 0, share, 1, 7),
+        (4, 0, half, 2, 2),
+        (4, half, half, 2, 6),
+        (1, 0, share, 3, 1),
+        (7, 0, share, 4, 7),
+    )
+    if not relay:
+        routes = tuple((d, 0, share, d - 1, d) for d in y_order)
+    copies = [
+        send(
+            part_ref.at[share_of(d, start, size)],
+            rs_slots.at[slot, pl.ds(start, size)],
+            y_send.at[0, at],
+            y_recv.at[0, at],
+            along_y(to),
+        )
+        for at, (d, start, size, slot, to) in enumerate(routes)
+    ]
 
     brought[2].wait()
     brought[3].wait()
@@ -238,7 +264,19 @@
     kept = jnp.where(live, weight_ref[...], 0.0)
     wgt[...] = jnp.zeros_like(wgt)
     wgt[:NBR, :rows] = kept
-    build_weights(rows, idx, wgt, w_hi, w_lo)
+    build_weights(rows, 1, idx, wgt, w_hi, w_lo)
+    if relay:
+        for copy in copies[:4]:
+            copy.wait_recv()
+        turn[0] = part_ref[share_of(2), :] + rs_slots[0]
+        turn[0, :half] += rs_slots[2, :half]
+        turn[1] = part_ref[share_of(6), :] + rs_slots[1]
+        turn[1, half:] += rs_slots[2, half:]
+        copies = copies[4:] + [
+            send(turn.at[at], rs_slots.at[5 + at], y_send.at[0, 6 + at], y_recv.at[0, 6 + at], to)
+            for at, to in enumerate((along_y(2), along_y(6)))
+        ]
+    build_weights(rows, 0, idx, wgt, w_hi, w_lo)
     inverse = 1.0 / (1.0 + jnp.sum(wgt[...], axis=0, keepdims=True))
     brought[4].wait()
     cents = centroid_ref[...]
@@ -257,9 +295,9 @@
     hot = onehot.astype(BF16)
 
     value = part_ref[own, :]
-    for d, copy in zip(y_order, copies):
+    for at, copy in enumerate(copies):
         copy.wait_recv()
-        value += rs_slots[d - 1]
+        value += rs_slots[3 + at if relay else y_order[at] - 1]
 
     def spread(field, block):
         hi, lo = split2(field)
@@ -276,6 +314,8 @@
             state.at[step], halo.at[step, 1], h_send.at[step, 1], h_recv.at[step, 1], before
         )
         total = value + spread(value, 1)
+        if step == 0:
+            build_weights(rows, 2, idx, wgt, w_hi, w_lo)
         up.wait_recv()
         total += spread(halo[step, 0], 0)
         down.wait_recv()
@@ -283,18 +323,30 @@
         value = total * inverse
 
     full[own, :] = value
-    copies = []
-    for d in y_order:
-        copies.append(
-            send(full.at[own], full.at[own], y_send.at[1, d - 1], y_recv.at[1, d - 1], along_y(d))
-        )
-    smooth_ref[...] = value[:, :rows]
+
+    def share_to(target, at, rows_at):
+        return send(full.at[rows_at], full.at[rows_at], y_send.at[1, at], y_recv.at[1, at], target)
+
+    smooth_v[...] = value[:, :rows]
+    if relay:
+        near = [share_to(along_y(d), at, own) for at, d in enumerate((2, 6, 1, 7))]
+        near[0].wait_recv()
+        near.append(share_to(along_y(2), 4, share_of(6, half, half)))
+        near.append(share_to(along_y(1), 5, share_of(6)))
+        near[1].wait_recv()
+        near.append(share_to(along_y(6), 6, share_of(2, 0, half)))
+        near.append(share_to(along_y(7), 7, share_of(2)))
+        copies = near[2:]
+    else:
+        copies = [share_to(along_y(d), d - 1, own) for d in y_order]
+    smooth_copy = pltpu.make_async_copy(smooth_v, smooth_ref, o_sem.at[0])
+    smooth_copy.start()
     for copy in copies:
         copy.wait_recv()
 
     whole = full[...]
     norm = jnp.sqrt(jnp.sum(whole * whole, axis=0, keepdims=True) + EPSILON)
-    unit[...] = (whole / norm).astype(BF16)
+    unit[...] = (whole * (1.0 / norm)).astype(BF16)
 
     def kernel_rows(start):
         scores = dot(cent_ref[pl.ds(start, chunk), :], unit[...])
@@ -311,9 +363,9 @@
 
     sums = lax.fori_loop(0, n_gene, first, jnp.zeros((1, wide), F32))
     mine = pl.multiple_of(gene * chunk, chunk)
-    kernel_own = kernel_rows(mine)
-    hi, lo = split2(kernel_own / sums)
-    observed = dot_nt(hot, hi) + dot_nt(hot, lo)
+    kept_hi, kept_lo = k_hi[pl.ds(mine, chunk), :], k_lo[pl.ds(mine, chunk), :]
+    hi, lo = split2(onehot / sums)
+    observed = dot_nt(hi, kept_hi) + dot_nt(lo, kept_hi) + dot_nt(hi, kept_lo)
     column = lax.broadcasted_iota(jnp.int32, (B, chunk), 1) + gene * chunk
     fo_own[...] = jnp.where(column == n_gene * chunk - 1, counts, observed)
 
@@ -372,7 +424,8 @@
     lane = lax.broadcasted_iota(jnp.int32, (1, wide), 1)
     weighted = jnp.where(lane < rows, weighted, 1.0)
     factor = dot_tn(penalty_of(fo_all[gene]), jnp.concatenate([hot, hot, hot], axis=0))
-    response = (kernel_own * factor / weighted).astype(BF16)
+    kernel_own = kept_hi.astype(F32) + kept_lo.astype(F32)
+    response = (kernel_own * factor * (1.0 / weighted)).astype(BF16)
     cs[...] = dot_nt(response, unit[...])
     fb_own[...] = dot_nt(hot, response)
 
@@ -412,6 +465,19 @@
                 along_y(d),
             )
         )
+
+    def piece_to(d, e, target):
+        rows_at = (lax.rem(gene + n_gene - d, n_gene), inner)
+        return send(
+            new_cent_ref.at[rows_at],
+            new_cent_ref.at[rows_at],
+            x_send.at[e, d],
+            x_recv.at[e, d],
+            target,
+        )
+
+    x_order = farthest_first(n_x)
+    x_copies = [[piece_to(0, e, along_in(2 * e))] for e in x_order]
     obs_ref[gene] = fb_second()
     obs_copies = []
     for d in y_order:
@@ -424,41 +490,72 @@
                 along_y(d),
             )
         )
-    for copy in copies:
+    for d, copy in reversed(list(zip(y_order, copies))):
         copy.wait_recv()
-
-    def column(number, target, sems, at):
-        send_sem, recv_sem = sems
-        return send(
-            new_cent_ref.at[:, number],
-            new_cent_ref.at[:, number],
-            send_sem.at[at],
-            recv_sem.at[at],
-            target,
-        )
-
-    x_order = farthest_first(n_x)
-    copies = [column(inner, along_in(2 * e), (c_send.at[2], c_recv.at[2]), e) for e in x_order]
-    shared = [column(inner, twin, (t_send, t_recv), 0)]
-    for e, copy in zip(x_order, copies):
-        copy.wait_recv()
+        for e, group in zip(x_order, x_copies):
+            group.append(piece_to(d, e, along_in(2 * e)))
+
+    out_copies = [smooth_copy]
+
+    def keep(number, at):
+        copy = pltpu.make_async_copy(
+            new_cent_ref.at[:, number], cent_out.at[:, number], o_sem.at[at]
+        )
+        copy.start()
+        out_copies.append(copy)
+
+    def to_twin(number, at):
+        column = new_cent_ref.at[:, number]
+        return send(column, column, t_send.at[at], t_recv.at[at], twin)
+
+    shared = [to_twin(inner, 0)]
+    keep(inner, 1)
+    for e, group in zip(x_order, x_copies):
+        for copy in group:
+            copy.wait_recv()
         number = lax.rem(inner + n_in - 2 * e, n_in)
-        shared.append(column(number, twin, (t_send, t_recv), e))
+        shared.append(to_twin(number, e))
+        keep(number, 1 + e)
     for copy in obs_copies:
         copy.wait_recv()
     for at in range(n_gene):
         size = min(chunk, k_real - at * chunk)
-        obs_out[:, at * chunk : at * chunk + size] = obs_ref[at][:, :size]
-    for copy in shared:
+        obs_v[:, at * chunk : at * chunk + size] = obs_ref[at][:, :size]
+    obs_copy = pltpu.make_async_copy(obs_v, obs_out, o_sem.at[1 + n_in])
+    obs_copy.start()
+    out_copies.append(obs_copy)
+    other = inner + 1 - 2 * core
+    for e, copy in zip([0] + x_order, shared):
         copy.wait_recv()
-    for at in range(n_gene):
-        for part in range(n_in):
-            start = at * chunk + part * piece
-            size = min(piece, k_real - start)
-            if size > 0:
-                cent_out[start : start + size, :] = new_cent_ref[at, part][:size]
+        keep(lax.rem(other + n_in - 2 * e, n_in), 1 + n_x + e)
+    for copy in out_copies:
+        copy.wait()
     for copy in pending:
         copy.wait_send()
+
+
+def results_kernel(
+    smooth_ref, cent_ref, obs_ref, smooth_out, cent_out, obs_out, smooth_v, cent_v, obs_v, sem
+):
+    k_real = cent_out.shape[0]
+    parts = 4
+    step = padded(-(-k_real // parts), 8)
+    spans = [pl.ds(at * step, min(step, k_real - at * step)) for at in range(parts)]
+    routes = [(cent_ref.at[span], cent_v.at[span], cent_out.at[span]) for span in spans]
+    routes += [(smooth_ref, smooth_v, smooth_out), (obs_ref, obs_v, obs_out)]
+    arriving = [
+        pltpu.make_async_copy(a, b, sem.at[0, at]) for at, (a, b, _) in enumerate(routes)
+    ]
+    leaving = [
+        pltpu.make_async_copy(b, c, sem.at[1, at]) for at, (_, b, c) in enumerate(routes)
+    ]
+    for copy in arriving:
+        copy.start()
+    for before, after in zip(arriving, leaving):
+        before.wait()
+        after.start()
+    for copy in leaving:
+        copy.wait()
 
 
 def shards(n_in, expression, gene_mean, loadings, nbr_index, nbr_count, nbr_weight, batch, centroids):
@@ -480,11 +577,11 @@
         functools.partial(main_kernel, dims),
         out_shape=[
             jax.ShapeDtypeStruct((share, rows), F32),
-            jax.ShapeDtypeStruct((k_real, comps), F32),
+            jax.ShapeDtypeStruct((n_gene, n_in, piece, comps), F32),
             jax.ShapeDtypeStruct((B, k_real), F32),
         ],
         in_specs=[hbm, vmem, hbm, hbm, vmem, hbm, vmem, hbm],
-        out_specs=[vmem] * 3,
+        out_specs=[hbm] * 3,
         scratch_shapes=[
             pltpu.VMEM((n_gene, n_in, piece, comps), F32),
             pltpu.VMEM((n_gene, B, chunk), F32),
@@ -508,21 +605,21 @@
             pltpu.VMEM((k_wide, wide), BF16),
             pltpu.VMEM((k_wide, wide), BF16),
             pltpu.VMEM((B, chunk), F32),
-            pltpu.VMEM((n_in - 1, B, chunk), F32),
+            pltpu.VMEM((max(n_in - 1, 1), B, chunk), F32),
             pltpu.VMEM((B, chunk), F32),
-            pltpu.VMEM((n_out - 1, B, chunk), F32),
+            pltpu.VMEM((max(n_out - 1, 1), B, chunk), F32),
             pltpu.VMEM((n_gene, B, chunk), F32),
             pltpu.VMEM((3 * B, k_wide), BF16),
             pltpu.VMEM((chunk, comps), F32),
-            pltpu.VMEM((n_in - 1, piece, comps), F32),
+            pltpu.VMEM((max(n_in - 1, 1), piece, comps), F32),
             pltpu.VMEM((piece, comps), F32),
-            pltpu.VMEM((n_out - 1, piece, comps), F32),
+            pltpu.VMEM((max(n_out - 1, 1), piece, comps), F32),
             pltpu.VMEM((B, chunk), F32),
-            pltpu.VMEM((n_in - 1, B, chunk), F32),
+            pltpu.VMEM((max(n_in - 1, 1), B, chunk), F32),
             pltpu.VMEM((B, chunk), F32),
-            pltpu.VMEM((n_out - 1, B, chunk), F32),
-            dma((6, n_gene - 1)),
-            dma((6, n_gene - 1)),
+            pltpu.VMEM((max(n_out - 1, 1), B, chunk), F32),
+            dma((6, n_gene)),
+            dma((6, n_gene)),
             dma((DIFF_STEPS, 2)),
             dma((DIFF_STEPS, 2)),
             dma((4, max(n_in, n_out) - 1)),
@@ -531,6 +628,12 @@
             dma((3, max(n_in, n_out) - 1)),
             dma((n_in // 2,)),
             dma((n_in // 2,)),
+            dma((n_in // 2, n_gene)),
+            dma((n_in // 2, n_gene)),
+            dma((n_in + 2,)),
+            pltpu.VMEM((2, share, wide), F32),
+            pltpu.VMEM((share, rows), F32),
+            pltpu.VMEM((B, k_real), F32),
         ],
         compiler_params=pltpu.CompilerParams(
             collective_id=0, has_side_effects=True, vmem_limit_bytes=60 * 1024 * 1024
@@ -546,6 +649,23 @@
         centroids,
     )
 
+    smooth, new_cent, obs = pl.pallas_call(
+        results_kernel,
+        out_shape=[
+            jax.ShapeDtypeStruct((share, rows), F32),
+            jax.ShapeDtypeStruct((k_real, comps), F32),
+            jax.ShapeDtypeStruct((B, k_real), F32),
+        ],
+        in_specs=[hbm] * 3,
+        out_specs=[hbm] * 3,
+        scratch_shapes=[
+            pltpu.VMEM((share, rows), F32),
+            pltpu.VMEM((k_real, comps), F32),
+            pltpu.VMEM((B, k_real), F32),
+            dma((2, 6)),
+        ],
+        compiler_params=pltpu.CompilerParams(vmem_limit_bytes=60 * 1024 * 1024),
+    )(smooth, new_cent.reshape(k_wide, comps), obs)
     return (smooth.T, new_cent, obs.T)
 
 
@@ -561,6 +681,6 @@
         P(),
     )
     out_specs = (P("cell", "gene"), P(), P())
-    n_in = 8 if mesh.shape["cell"] % 64 == 0 else 4
+    n_in = min(8, mesh.shape["cell"])
     body = functools.partial(shards, n_in)
     return jax.shard_map(body, mesh=mesh, in_specs=in_specs, out_specs=out_specs, check_vma=False)

time: 109 us -> 96.5 us (0.89)
  Pallas kernels: 104 us -> 95.6 us
  local copies, waits for them, and re-layouts: 4.43 us -> 0 us
    pallas_call x1, Pallas kernels: 104 us -> 93.6 us  [shards(): pl.pallas_call(functools.partial(main_kernel, dims), out_shape=[jax.Shape...]
    unnamed x5 -> x0, local copies, waits for them, and re-layouts: 4.43 us -> none
    pallas_call x0 -> x1, Pallas kernels: none -> 2.05 us  [shards(): pl.pallas_call(results_kernel, out_shape=[jax.ShapeDtypeStruct((share, ro...]
where the time goes in v3:
time: 96.5 us; the launch traced here: 96.3 us
  Pallas kernels  95.6 us (99%)
    pallas_call x1, Pallas kernels, shards(): pl.pallas_call(functools.partial(main_kernel, dims), out_shape=[jax.Shape...  93.6 us
    pallas_call x1, Pallas kernels, shards(): pl.pallas_call(results_kernel, out_shape=[jax.ShapeDtypeStruct((share, ro...  2.05 us

profile of v3, /device:TPU:1, one launch (start us, length us, event | category | flops | bytes accessed | tf_op | source)
XLA Modules:
  0.0 96.3 jit_solution(11268843501639393369)
XLA Ops:
  0.6 93.6 %shard_map.103 = (f32[32,576]{1,0:T(8,128)}, f32[8,8,16,256]{3,2,1,0:T(8,128)}, f32[16,1000]{1,0:T(8,128)}) custom-call(bf16[576,512]{1,0:T(8,128)(2,1)} %expr_hbm.1, f32[512]{0:T(512)} %mean_ref.1, bf16[512,256]{1,0:T(8,128)(2,1)} %load_hbm.1, s32[30,576]{1,0:T(8,128)} %bitcast.6, s32[576]{0:T(1024)} %count_ref.1, f32[30,576]{1,0:T(8,128)} %bitcast.7, ...), custom_call_target="tpu_custom_call" | custom-call | tf_op jit(solution)/shard_map/pallas_call | solution.py:576
  94.2 2.0 %shard_map.104 = (f32[32,576]{1,0:T(8,128)}, f32[1000,256]{1,0:T(8,128)}, f32[16,1000]{1,0:T(8,128)}) custom-call(f32[32,576]{1,0:T(8,128)} %get-tuple-element.9.smooth_ref, f32[1024,256]{1,0:T(8,128)} %bitcast.5, f32[16,1000]{1,0:T(8,128)} %get-tuple-element.11.obs_ref), custom_call_target="tpu_custom_call" | custom-call | tf_op jit(solution)/shard_map/pallas_call | solution.py:652

commit v4 on v3

--- a/solution.py
+++ b/solution.py
@@ -50,17 +50,19 @@
     return sorted(range(1, count), key=lambda d: -min(d, count - d))
 
 
-def build_weights(rows, block, index_ref, weight_ref, hi_ref, lo_ref):
+def build_weights(rows, block, index_ref, weight_ref, hi_ref, lo_ref, places=None):
     wide = hi_ref.shape[1]
     tile = LANE
     tiles = wide // tile
     base = block * wide
-    span = slice(base, base + wide)
-    hi_ref[span, :] = jnp.zeros((wide, wide), BF16)
-    lo_ref[span, :] = jnp.zeros((wide, wide), BF16)
-    for at in range(tiles):
+    for at in places or range(tiles):
         lanes = slice(at * tile, (at + 1) * tile)
         first, last = ((at, tiles), (0, tiles), (0, at + 1))[block]
+        for low, high in ((0, first * tile), (min(last * tile, rows), wide)):
+            if low < high:
+                empty = jnp.zeros((high - low, tile), BF16)
+                hi_ref[base + low : base + high, lanes] = empty
+                lo_ref[base + low : base + high, lanes] = empty
 
         def rows_of(start, height, lanes=lanes):
             source = lax.broadcasted_iota(jnp.int32, (height, tile), 0) + (
@@ -69,7 +71,7 @@
             total = jnp.zeros((height, tile), F32)
             for slot in range(NBR):
                 hit = index_ref[slot : slot + 1, lanes] == source
-                total += jnp.where(hit, weight_ref[slot : slot + 1, lanes], 0.0)
+                total = jnp.where(hit, weight_ref[slot : slot + 1, lanes], total)
             hi, lo = split2(total)
             hi_ref[pl.ds(base + start, height), lanes] = hi
             lo_ref[pl.ds(base + start, height), lanes] = lo
@@ -94,9 +96,8 @@
     batch_ref,
     centroid_hbm,
     smooth_ref,
-    cent_out,
+    new_cent_ref,
     obs_out,
-    new_cent_ref,
     obs_ref,
     expr_ref,
     load_ref,
@@ -143,10 +144,7 @@
     t_recv,
     x_send,
     x_recv,
-    o_sem,
     turn,
-    smooth_v,
-    obs_v,
 ):
     rows, k_real, n_gene, n_in, n_out = dims
     n_cell = n_in * n_out
@@ -245,16 +243,19 @@
     )
     if not relay:
         routes = tuple((d, 0, share, d - 1, d) for d in y_order)
-    copies = [
-        send(
+    early = 4 if relay else len(routes)
+
+    def send_route(at):
+        d, start, size, slot, to = routes[at]
+        return send(
             part_ref.at[share_of(d, start, size)],
             rs_slots.at[slot, pl.ds(start, size)],
             y_send.at[0, at],
             y_recv.at[0, at],
             along_y(to),
         )
-        for at, (d, start, size, slot, to) in enumerate(routes)
-    ]
+
+    copies = [send_route(at) for at in range(early)]
 
     brought[2].wait()
     brought[3].wait()
@@ -264,7 +265,15 @@
     kept = jnp.where(live, weight_ref[...], 0.0)
     wgt[...] = jnp.zeros_like(wgt)
     wgt[:NBR, :rows] = kept
-    build_weights(rows, 1, idx, wgt, w_hi, w_lo)
+    inverse = 1.0 / (1.0 + jnp.sum(wgt[...], axis=0, keepdims=True))
+    merged = jnp.zeros(wgt.shape, F32)
+    for slot in range(NBR):
+        same = idx[...] == idx[slot : slot + 1, :]
+        merged += jnp.where(same, wgt[slot : slot + 1, :], 0.0)
+    wgt[...] = merged
+    build_weights(rows, 1, idx, wgt, w_hi, w_lo, range(2))
+    copies += [send_route(at) for at in range(early, len(routes))]
+    build_weights(rows, 1, idx, wgt, w_hi, w_lo, range(2, wide // LANE))
     if relay:
         for copy in copies[:4]:
             copy.wait_recv()
@@ -277,7 +286,6 @@
             for at, to in enumerate((along_y(2), along_y(6)))
         ]
     build_weights(rows, 0, idx, wgt, w_hi, w_lo)
-    inverse = 1.0 / (1.0 + jnp.sum(wgt[...], axis=0, keepdims=True))
     brought[4].wait()
     cents = centroid_ref[...]
     cent_norm = jnp.sqrt(jnp.sum(cents * cents, axis=1, keepdims=True) + EPSILON)
@@ -301,9 +309,16 @@
 
     def spread(field, block):
         hi, lo = split2(field)
-        span = slice(block * wide, (block + 1) * wide)
-        both = dot(jnp.concatenate([hi, lo], axis=0), w_hi[span, :])
-        return both[:share] + both[share:] + dot(hi, w_lo[span, :])
+        pair = jnp.concatenate([hi, lo], axis=0)
+        base = block * wide
+        found = []
+        for low in range(0, wide, 2 * LANE):
+            high = min(low + 2 * LANE, wide)
+            first, last = ((low, wide), (0, wide), (0, high))[block]
+            span, lanes = slice(base + first, base + last), slice(low, high)
+            both = dot(pair[:, first:last], w_hi[span, lanes])
+            found.append(both[:share] + both[share:] + dot(hi[:, first:last], w_lo[span, lanes]))
+        return jnp.concatenate(found, axis=1)
 
     for step in range(DIFF_STEPS):
         state[step] = value
@@ -324,44 +339,57 @@
 
     full[own, :] = value
 
-    def share_to(target, at, rows_at):
-        return send(full.at[rows_at], full.at[rows_at], y_send.at[1, at], y_recv.at[1, at], target)
-
-    smooth_v[...] = value[:, :rows]
+    cut = padded(wide * 3 // 5)
+    spans = ((0, cut), (cut, wide - cut))
+
+    def share_to(target, at, rows_at, part):
+        place = full.at[rows_at, pl.ds(*spans[part])]
+        return send(place, place, y_send.at[1 + 4 * part, at], y_recv.at[1 + 4 * part, at], target)
+
+    smooth_ref[...] = value[:, :rows]
     if relay:
-        near = [share_to(along_y(d), at, own) for at, d in enumerate((2, 6, 1, 7))]
-        near[0].wait_recv()
-        near.append(share_to(along_y(2), 4, share_of(6, half, half)))
-        near.append(share_to(along_y(1), 5, share_of(6)))
-        near[1].wait_recv()
-        near.append(share_to(along_y(6), 6, share_of(2, 0, half)))
-        near.append(share_to(along_y(7), 7, share_of(2)))
-        copies = near[2:]
+        near = [
+            [share_to(along_y(d), at, own, part) for at, d in enumerate((2, 6, 1, 7))]
+            for part in range(2)
+        ]
+        arrivals = []
+        for part in range(2):
+            one, two = near[part][:2]
+            one.wait_recv()
+            far = [
+                share_to(along_y(2), 4, share_of(6, half, half), part),
+                share_to(along_y(1), 5, share_of(6), part),
+            ]
+            two.wait_recv()
+            far.append(share_to(along_y(6), 6, share_of(2, 0, half), part))
+            far.append(share_to(along_y(7), 7, share_of(2), part))
+            arrivals.append(near[part][2:] + far)
     else:
-        copies = [share_to(along_y(d), d - 1, own) for d in y_order]
-    smooth_copy = pltpu.make_async_copy(smooth_v, smooth_ref, o_sem.at[0])
-    smooth_copy.start()
-    for copy in copies:
-        copy.wait_recv()
-
-    whole = full[...]
-    norm = jnp.sqrt(jnp.sum(whole * whole, axis=0, keepdims=True) + EPSILON)
-    unit[...] = (whole * (1.0 / norm)).astype(BF16)
-
-    def kernel_rows(start):
-        scores = dot(cent_ref[pl.ds(start, chunk), :], unit[...])
-        number = lax.broadcasted_iota(jnp.int32, (chunk, wide), 0) + start
-        return jnp.where(number < k_real, jnp.exp((scores - 1.0) * (2.0 / SIGMA_SCALE)), 0.0)
-
-    def first(at, sums):
-        start = pl.multiple_of(at * chunk, chunk)
-        values = kernel_rows(start)
-        hi, lo = split2(values)
-        k_hi[pl.ds(start, chunk), :] = hi
-        k_lo[pl.ds(start, chunk), :] = lo
-        return sums + jnp.sum(values, axis=0, keepdims=True)
-
-    sums = lax.fori_loop(0, n_gene, first, jnp.zeros((1, wide), F32))
+        arrivals = [[share_to(along_y(d), d - 1, own, part) for d in y_order] for part in range(2)]
+
+    found = []
+    for part in range(2):
+        low, size = spans[part]
+        lanes = slice(low, low + size)
+        for copy in arrivals[part]:
+            copy.wait_recv()
+        whole = full[:, lanes]
+        norm = jnp.sqrt(jnp.sum(whole * whole, axis=0, keepdims=True) + EPSILON)
+        unit[:, lanes] = (whole * (1.0 / norm)).astype(BF16)
+
+        def first(at, sums, lanes=lanes, size=size):
+            start = pl.multiple_of(at * chunk, chunk)
+            scores = dot(cent_ref[pl.ds(start, chunk), :], unit[:, lanes])
+            number = lax.broadcasted_iota(jnp.int32, (chunk, size), 0) + start
+            values = jnp.exp((scores - 1.0) * (2.0 / SIGMA_SCALE))
+            values = jnp.where(number < k_real, values, 0.0)
+            hi, lo = split2(values)
+            k_hi[pl.ds(start, chunk), lanes] = hi
+            k_lo[pl.ds(start, chunk), lanes] = lo
+            return sums + jnp.sum(values, axis=0, keepdims=True)
+
+        found.append(lax.fori_loop(0, n_gene, first, jnp.zeros((1, size), F32)))
+    sums = jnp.concatenate(found, axis=1)
     mine = pl.multiple_of(gene * chunk, chunk)
     kept_hi, kept_lo = k_hi[pl.ds(mine, chunk), :], k_lo[pl.ds(mine, chunk), :]
     hi, lo = split2(onehot / sums)
@@ -441,13 +469,13 @@
                 along_in(d),
             )
         )
-    fb_first = all_sum(fb_own, fb_in, along_in, n_in, a_sems, 2)
     piece_sum = cs[pl.ds(pl.multiple_of(inner * piece, piece), piece), :]
     for d, copy in zip(in_order, c_copies):
         copy.wait_recv()
         piece_sum += cs_in[d - 1]
     cs_mid[...] = piece_sum
     cs_second = all_sum(cs_mid, cs_out, along_out, n_out, (c_send, c_recv), 1)
+    fb_first = all_sum(fb_own, fb_in, along_in, n_in, a_sems, 2)
     fb_mid[...] = fb_first()
     fb_second = all_sum(fb_mid, fb_out, along_out, n_out, a_sems, 3)
     piece_sum = cs_second()
@@ -495,66 +523,37 @@
         for e, group in zip(x_order, x_copies):
             group.append(piece_to(d, e, along_in(2 * e)))
 
-    out_copies = [smooth_copy]
-
-    def keep(number, at):
-        copy = pltpu.make_async_copy(
-            new_cent_ref.at[:, number], cent_out.at[:, number], o_sem.at[at]
-        )
-        copy.start()
-        out_copies.append(copy)
-
     def to_twin(number, at):
         column = new_cent_ref.at[:, number]
         return send(column, column, t_send.at[at], t_recv.at[at], twin)
 
     shared = [to_twin(inner, 0)]
-    keep(inner, 1)
     for e, group in zip(x_order, x_copies):
         for copy in group:
             copy.wait_recv()
         number = lax.rem(inner + n_in - 2 * e, n_in)
         shared.append(to_twin(number, e))
-        keep(number, 1 + e)
     for copy in obs_copies:
         copy.wait_recv()
     for at in range(n_gene):
         size = min(chunk, k_real - at * chunk)
-        obs_v[:, at * chunk : at * chunk + size] = obs_ref[at][:, :size]
-    obs_copy = pltpu.make_async_copy(obs_v, obs_out, o_sem.at[1 + n_in])
-    obs_copy.start()
-    out_copies.append(obs_copy)
-    other = inner + 1 - 2 * core
-    for e, copy in zip([0] + x_order, shared):
+        obs_out[:, at * chunk : at * chunk + size] = obs_ref[at][:, :size]
+    for copy in shared:
         copy.wait_recv()
-        keep(lax.rem(other + n_in - 2 * e, n_in), 1 + n_x + e)
-    for copy in out_copies:
-        copy.wait()
     for copy in pending:
         copy.wait_send()
 
 
-def results_kernel(
-    smooth_ref, cent_ref, obs_ref, smooth_out, cent_out, obs_out, smooth_v, cent_v, obs_v, sem
-):
-    k_real = cent_out.shape[0]
-    parts = 4
-    step = padded(-(-k_real // parts), 8)
-    spans = [pl.ds(at * step, min(step, k_real - at * step)) for at in range(parts)]
-    routes = [(cent_ref.at[span], cent_v.at[span], cent_out.at[span]) for span in spans]
-    routes += [(smooth_ref, smooth_v, smooth_out), (obs_ref, obs_v, obs_out)]
-    arriving = [
-        pltpu.make_async_copy(a, b, sem.at[0, at]) for at, (a, b, _) in enumerate(routes)
-    ]
-    leaving = [
-        pltpu.make_async_copy(b, c, sem.at[1, at]) for at, (_, b, c) in enumerate(routes)
-    ]
-    for copy in arriving:
+def results_kernel(smooth_ref, cent_ref, obs_ref, smooth_out, cent_out, obs_out, sem):
+    routes = (
+        (cent_ref.at[pl.ds(0, cent_out.shape[0])], cent_out),
+        (smooth_ref, smooth_out),
+        (obs_ref, obs_out),
+    )
+    copies = [pltpu.make_async_copy(a, b, sem.at[at]) for at, (a, b) in enumerate(routes)]
+    for copy in copies:
         copy.start()
-    for before, after in zip(arriving, leaving):
-        before.wait()
-        after.start()
-    for copy in leaving:
+    for copy in copies:
         copy.wait()
 
 
@@ -576,14 +575,13 @@
     smooth, new_cent, obs = pl.pallas_call(
         functools.partial(main_kernel, dims),
         out_shape=[
-            jax.ShapeDtypeStruct((share, rows), F32),
-            jax.ShapeDtypeStruct((n_gene, n_in, piece, comps), F32),
-            jax.ShapeDtypeStruct((B, k_real), F32),
+            pltpu.VMEM((share, rows), F32),
+            pltpu.VMEM((n_gene, n_in, piece, comps), F32),
+            pltpu.VMEM((B, k_real), F32),
         ],
         in_specs=[hbm, vmem, hbm, hbm, vmem, hbm, vmem, hbm],
-        out_specs=[hbm] * 3,
+        out_specs=[vmem] * 3,
         scratch_shapes=[
-            pltpu.VMEM((n_gene, n_in, piece, comps), F32),
             pltpu.VMEM((n_gene, B, chunk), F32),
             pltpu.VMEM(expression.shape, BF16),
             pltpu.VMEM(loadings.shape, BF16),
@@ -630,10 +628,7 @@
             dma((n_in // 2,)),
             dma((n_in // 2, n_gene)),
             dma((n_in // 2, n_gene)),
-            dma((n_in + 2,)),
             pltpu.VMEM((2, share, wide), F32),
-            pltpu.VMEM((share, rows), F32),
-            pltpu.VMEM((B, k_real), F32),
         ],
         compiler_params=pltpu.CompilerParams(
             collective_id=0, has_side_effects=True, vmem_limit_bytes=60 * 1024 * 1024
@@ -656,15 +651,10 @@
             jax.ShapeDtypeStruct((k_real, comps), F32),
             jax.ShapeDtypeStruct((B, k_real), F32),
         ],
-        in_specs=[hbm] * 3,
+        in_specs=[vmem] * 3,
         out_specs=[hbm] * 3,
-        scratch_shapes=[
-            pltpu.VMEM((share, rows), F32),
-            pltpu.VMEM((k_real, comps), F32),
-            pltpu.VMEM((B, k_real), F32),
-            dma((2, 6)),
-        ],
-        compiler_params=pltpu.CompilerParams(vmem_limit_bytes=60 * 1024 * 1024),
+        scratch_shapes=[dma((3,))],
+        compiler_params=pltpu.CompilerParams(vmem_limit_bytes=32 * 1024 * 1024),
     )(smooth, new_cent.reshape(k_wide, comps), obs)
     return (smooth.T, new_cent, obs.T)
 

time: 96.5 us -> 92.8 us (0.962)
  Pallas kernels: 95.6 us -> 91.9 us
    pallas_call x1, Pallas kernels: 93.6 us -> 90.9 us  [shards(): pl.pallas_call(functools.partial(main_kernel, dims), out_shape=[pltpu.VME...]
    pallas_call x1, Pallas kernels: 2.05 us -> 1.02 us  [shards(): pl.pallas_call(results_kernel, out_shape=[jax.ShapeDtypeStruct((share, ro...]
where the time goes in v4:
time: 92.8 us; the launch traced here: 92.6 us
  Pallas kernels  91.9 us (99%)
    pallas_call x1, Pallas kernels, shards(): pl.pallas_call(functools.partial(main_kernel, dims), out_shape=[pltpu.VME...  90.9 us

profile of v4, /device:TPU:1, one launch (start us, length us, event | category | flops | bytes accessed | tf_op | source)
XLA Modules:
  0.0 92.6 jit_solution(9148724145380831422)
XLA Ops:
  0.6 90.9 %shard_map.103 = (f32[32,576]{1,0:T(8,128)S(1)}, f32[8,8,16,256]{3,2,1,0:T(8,128)S(1)}, f32[16,1000]{1,0:T(8,128)S(1)}) custom-call(bf16[576,512]{1,0:T(8,128)(2,1)} %expr_hbm.1, f32[512]{0:T(512)} %mean_ref.1, bf16[512,256]{1,0:T(8,128)(2,1)} %load_hbm.1, s32[30,576]{1,0:T(8,128)} %bitcast.6, s32[576]{0:T(1024)} %count_ref.1, f32[30,576]{1,0:T(8,128)} %bitcast.7, ...), custom_call_target="tpu_custom_call" | custom-call | tf_op jit(solution)/shard_map/pallas_call | solution.py:575
  91.6 1.0 %shard_map.104 = (f32[32,576]{1,0:T(8,128)}, f32[1000,256]{1,0:T(8,128)}, f32[16,1000]{1,0:T(8,128)}) custom-call(f32[32,576]{1,0:T(8,128)S(1)} %get-tuple-element.9.smooth_ref, f32[1024,256]{1,0:T(8,128)S(1)} %bitcast.5, f32[16,1000]{1,0:T(8,128)S(1)} %get-tuple-element.11.obs_ref), custom_call_target="tpu_custom_call" | custom-call | tf_op jit(solution)/shard_map/pallas_call | solution.py:647

commit v5 on v4

--- a/solution.py
+++ b/solution.py
@@ -225,6 +225,10 @@
         pending.append(copy)
         return copy
 
+    def settle(latest):
+        while len(pending) > latest:
+            pending.pop(0).wait_send()
+
     half = share // 2
     relay = n_gene == 8
 
@@ -331,6 +335,7 @@
         total = value + spread(value, 1)
         if step == 0:
             build_weights(rows, 2, idx, wgt, w_hi, w_lo)
+        settle(2)
         up.wait_recv()
         total += spread(halo[step, 0], 0)
         down.wait_recv()
@@ -346,7 +351,6 @@
         place = full.at[rows_at, pl.ds(*spans[part])]
         return send(place, place, y_send.at[1 + 4 * part, at], y_recv.at[1 + 4 * part, at], target)
 
-    smooth_ref[...] = value[:, :rows]
     if relay:
         near = [
             [share_to(along_y(d), at, own, part) for at, d in enumerate((2, 6, 1, 7))]
@@ -367,6 +371,9 @@
     else:
         arrivals = [[share_to(along_y(d), d - 1, own, part) for d in y_order] for part in range(2)]
 
+    smooth_ref[...] = value[:, :rows]
+
+    settle(16 if relay else 2 * len(y_order))
     found = []
     for part in range(2):
         low, size = spans[part]
@@ -411,7 +418,8 @@
                 )
             )
 
-        def finish():
+        def finish(latest=count - 1):
+            settle(latest)
             total = source[...]
             for d, copy in zip(farthest_first(count), copies):
                 copy.wait_recv()
@@ -434,6 +442,7 @@
                 along_y(d),
             )
         )
+    settle(n_gene - 1)
     for copy in copies:
         copy.wait_recv()
 
@@ -469,6 +478,7 @@
                 along_in(d),
             )
         )
+    settle(n_in - 1)
     piece_sum = cs[pl.ds(pl.multiple_of(inner * piece, piece), piece), :]
     for d, copy in zip(in_order, c_copies):
         copy.wait_recv()
@@ -476,9 +486,9 @@
     cs_mid[...] = piece_sum
     cs_second = all_sum(cs_mid, cs_out, along_out, n_out, (c_send, c_recv), 1)
     fb_first = all_sum(fb_own, fb_in, along_in, n_in, a_sems, 2)
-    fb_mid[...] = fb_first()
+    fb_mid[...] = fb_first(n_in + n_out - 2)
     fb_second = all_sum(fb_mid, fb_out, along_out, n_out, a_sems, 3)
-    piece_sum = cs_second()
+    piece_sum = cs_second(2 * (n_out - 1))
     length = jnp.sqrt(jnp.sum(piece_sum * piece_sum, axis=1, keepdims=True) + EPSILON)
 
     new_cent_ref[gene, inner] = piece_sum / length
@@ -506,7 +516,7 @@
 
     x_order = farthest_first(n_x)
     x_copies = [[piece_to(0, e, along_in(2 * e))] for e in x_order]
-    obs_ref[gene] = fb_second()
+    obs_ref[gene] = fb_second(2 * n_gene + n_x)
     obs_copies = []
     for d in y_order:
         obs_copies.append(
@@ -528,6 +538,7 @@
         return send(column, column, t_send.at[at], t_recv.at[at], twin)
 
     shared = [to_twin(inner, 0)]
+    settle(n_gene * n_x)
     for e, group in zip(x_order, x_copies):
         for copy in group:
             copy.wait_recv()
@@ -538,10 +549,10 @@
     for at in range(n_gene):
         size = min(chunk, k_real - at * chunk)
         obs_out[:, at * chunk : at * chunk + size] = obs_ref[at][:, :size]
+    settle(len(shared))
     for copy in shared:
         copy.wait_recv()
-    for copy in pending:
-        copy.wait_send()
+    settle(0)
 
 
 def results_kernel(smooth_ref, cent_ref, obs_ref, smooth_out, cent_out, obs_out, sem):

time: 92.8 us -> 92.6 us (level)
  no operation moved by 1% of the time
where the time goes in v5:
time: 92.6 us; the launch traced here: 92.4 us
  Pallas kernels  91.7 us (99%)
    pallas_call x1, Pallas kernels, shards(): pl.pallas_call(functools.partial(main_kernel, dims), out_shape=[pltpu.VME...  90.7 us

profile of v5, /device:TPU:1, one launch (start us, length us, event | category | flops | bytes accessed | tf_op | source)
XLA Modules:
  0.0 92.4 jit_solution(4129063641520727796)
XLA Ops:
  0.6 90.7 %shard_map.103 = (f32[32,576]{1,0:T(8,128)S(1)}, f32[8,8,16,256]{3,2,1,0:T(8,128)S(1)}, f32[16,1000]{1,0:T(8,128)S(1)}) custom-call(bf16[576,512]{1,0:T(8,128)(2,1)} %expr_hbm.1, f32[512]{0:T(512)} %mean_ref.1, bf16[512,256]{1,0:T(8,128)(2,1)} %load_hbm.1, s32[30,576]{1,0:T(8,128)} %bitcast.6, s32[576]{0:T(1024)} %count_ref.1, f32[30,576]{1,0:T(8,128)} %bitcast.7, ...), custom_call_target="tpu_custom_call" | custom-call | tf_op jit(solution)/shard_map/pallas_call | solution.py:586
  91.4 1.0 %shard_map.104 = (f32[32,576]{1,0:T(8,128)}, f32[1000,256]{1,0:T(8,128)}, f32[16,1000]{1,0:T(8,128)}) custom-call(f32[32,576]{1,0:T(8,128)S(1)} %get-tuple-element.9.smooth_ref, f32[1024,256]{1,0:T(8,128)S(1)} %bitcast.5, f32[16,1000]{1,0:T(8,128)S(1)} %get-tuple-element.11.obs_ref), custom_call_target="tpu_custom_call" | custom-call | tf_op jit(solution)/shard_map/pallas_call | solution.py:658

commit v6 on v5

--- a/solution.py
+++ b/solution.py
@@ -238,16 +238,18 @@
 
     own = share_of(0)
     routes = (
-        (3, 0, share, 0, 1),
-        (5, 0, share, 1, 7),
+        (3, 0, half, 0, 1),
+        (5, 0, half, 1, 7),
         (4, 0, half, 2, 2),
+        (3, half, half, 0, 1),
+        (5, half, half, 1, 7),
         (4, half, half, 2, 6),
         (1, 0, share, 3, 1),
         (7, 0, share, 4, 7),
     )
     if not relay:
         routes = tuple((d, 0, share, d - 1, d) for d in y_order)
-    early = 4 if relay else len(routes)
+    early = 6 if relay else len(routes)
 
     def send_route(at):
         d, start, size, slot, to = routes[at]
@@ -277,18 +279,31 @@
     wgt[...] = merged
     build_weights(rows, 1, idx, wgt, w_hi, w_lo, range(2))
     copies += [send_route(at) for at in range(early, len(routes))]
+
+    def pass_on(part):
+        for copy in copies[3 * part : 3 * part + 3]:
+            copy.wait_recv()
+        start = part * half
+        place = slice(start, start + half)
+        for at, d in enumerate((2, 6)):
+            turn[at, place] = part_ref[share_of(d, start, half), :] + rs_slots[at, place]
+        turn[part, place] += rs_slots[2, place]
+        return [
+            send(
+                turn.at[at, pl.ds(start, half)],
+                rs_slots.at[5 + at, pl.ds(start, half)],
+                y_send.at[6, 2 * part + at],
+                y_recv.at[6, 2 * part + at],
+                along_y(d),
+            )
+            for at, d in enumerate((2, 6))
+        ]
+
+    passed = pass_on(0) if relay else []
     build_weights(rows, 1, idx, wgt, w_hi, w_lo, range(2, wide // LANE))
     if relay:
-        for copy in copies[:4]:
-            copy.wait_recv()
-        turn[0] = part_ref[share_of(2), :] + rs_slots[0]
-        turn[0, :half] += rs_slots[2, :half]
-        turn[1] = part_ref[share_of(6), :] + rs_slots[1]
-        turn[1, half:] += rs_slots[2, half:]
-        copies = copies[4:] + [
-            send(turn.at[at], rs_slots.at[5 + at], y_send.at[0, 6 + at], y_recv.at[0, 6 + at], to)
-            for at, to in enumerate((along_y(2), along_y(6)))
-        ]
+        passed += pass_on(1)
+        copies = copies[6:] + passed
     build_weights(rows, 0, idx, wgt, w_hi, w_lo)
     brought[4].wait()
     cents = centroid_ref[...]
@@ -307,9 +322,10 @@
     hot = onehot.astype(BF16)
 
     value = part_ref[own, :]
-    for at, copy in enumerate(copies):
+    for copy in copies:
         copy.wait_recv()
-        value += rs_slots[3 + at if relay else y_order[at] - 1]
+    for slot in range(3 if relay else 0, n_gene - 1):
+        value += rs_slots[slot]
 
     def spread(field, block):
         hi, lo = split2(field)
@@ -627,8 +643,8 @@
             pltpu.VMEM((max(n_in - 1, 1), B, chunk), F32),
             pltpu.VMEM((B, chunk), F32),
             pltpu.VMEM((max(n_out - 1, 1), B, chunk), F32),
-            dma((6, n_gene)),
-            dma((6, n_gene)),
+            dma((7, n_gene)),
+            dma((7, n_gene)),
             dma((DIFF_STEPS, 2)),
             dma((DIFF_STEPS, 2)),
             dma((4, max(n_in, n_out) - 1)),

time: 92.6 us -> 92.7 us (level)
  no operation moved by 1% of the time
where the time goes in v6:
time: 92.7 us; the launch traced here: 92.5 us
  Pallas kernels  91.9 us (99%)
    pallas_call x1, Pallas kernels, shards(): pl.pallas_call(functools.partial(main_kernel, dims), out_shape=[pltpu.VME...  90.8 us

profile of v6, /device:TPU:1, one launch (start us, length us, event | category | flops | bytes accessed | tf_op | source)
XLA Modules:
  0.0 92.5 jit_solution(7801408837196453036)
XLA Ops:
  0.6 90.8 %shard_map.103 = (f32[32,576]{1,0:T(8,128)S(1)}, f32[8,8,16,256]{3,2,1,0:T(8,128)S(1)}, f32[16,1000]{1,0:T(8,128)S(1)}) custom-call(bf16[576,512]{1,0:T(8,128)(2,1)} %expr_hbm.1, f32[512]{0:T(512)} %mean_ref.1, bf16[512,256]{1,0:T(8,128)(2,1)} %load_hbm.1, s32[30,576]{1,0:T(8,128)} %bitcast.6, s32[576]{0:T(1024)} %count_ref.1, f32[30,576]{1,0:T(8,128)} %bitcast.7, ...), custom_call_target="tpu_custom_call" | custom-call | tf_op jit(solution)/shard_map/pallas_call | solution.py:602
  91.5 1.0 %shard_map.104 = (f32[32,576]{1,0:T(8,128)}, f32[1000,256]{1,0:T(8,128)}, f32[16,1000]{1,0:T(8,128)}) custom-call(f32[32,576]{1,0:T(8,128)S(1)} %get-tuple-element.9.smooth_ref, f32[1024,256]{1,0:T(8,128)S(1)} %bitcast.5, f32[16,1000]{1,0:T(8,128)S(1)} %get-tuple-element.11.obs_ref), custom_call_target="tpu_custom_call" | custom-call | tf_op jit(solution)/shard_map/pallas_call | solution.py:674
